TPU v7x, 32 devices: a whole 2x2x4 slice. The times are simulated.
32 devices in a mesh: segment: 4 (over z), blk: 8 (over y, x, core).
Axes of the slice: x: 2, y: 2, z: 4, core: 2. Of those that a mesh axis runs over, the one named last changes fastest.
Arguments:
- layer_inputs: bfloat16 [4, 6, 1024, 256], P('segment', None, 'blk'), may hold values from -6 to 6
- final_cot: bfloat16 [6, 1024, 256], P(None, 'blk'), may hold values from -6 to 6
- attn_weights: bfloat16 [4, 4, 256, 256], P('segment'), may hold values from -0.375 to 0.375
- norm_gain: float32 [4, 256], P('segment'), may hold values from 0.5 to 1.5
- pair_list: int32 [8, 4], replicated, may hold values from 0 to 7, as said below
- pair_count: int32 [8], replicated, may hold values from 2 to 4, as said below
Outputs:
- layer_cots: bfloat16 [4, 6, 1024, 256], P('segment', None, 'blk')
- weight_grads: float32 [4, 4, 256, 256], P('segment')
- gain_grads: float32 [4, 256], P('segment')
Inputs may be any that keep to these rules, and one draw needn't show every extreme that they name: `pair_list`: each row holds 4 distinct blocks and its first entry is the row's own block. `pair_count`: some row uses all 4 slots.
All inputs are finite; a program needn't handle non-finite values.
Results may differ from a plain program's by a relative error of at most 0.038.
Values may be sent and summed in bfloat16 or wider, within the bound.
No kernel may reach another device: no remote copies, remote signals or barrier semaphores. Data moves between devices by JAX's collectives and lax.ppermute only.
A program may use at most 64 MiB of HBM per device.

v0:
```python
from functools import partial

import jax
import jax.numpy as jnp
from jax import lax
from jax.sharding import PartitionSpec as P

HEADS = 16


eps = 1e-05
head_group = 4


def shifted(value, axis, steps):
    count = lax.axis_size(axis)
    initial, last = (max(0, -steps), min(count, count - steps))
    return lax.ppermute(value, axis, [(source, source + steps) for source in range(initial, last)])


def rms_parts(inputs, gain_row):
    feats = inputs.astype(jnp.float32)
    inv_rms = lax.rsqrt(jnp.mean(feats * feats, axis=-1, keepdims=True) + eps)
    unit_feat = feats * inv_rms
    normed = (unit_feat * gain_row).astype(jnp.bfloat16)
    return (unit_feat, inv_rms, normed)


def norm_back(normed_grad, unit_feat, inv_rms, gain_row):
    unit_grad = normed_grad * gain_row
    centre = jnp.mean(unit_grad * unit_feat, axis=-1, keepdims=True)
    return inv_rms * (unit_grad - unit_feat * centre)


def to_groups(values, head_size):
    lead = values.shape[:-1]
    grouped = values.reshape(lead + (-1, head_group, head_size))
    return jnp.moveaxis(grouped, len(lead), 0)


def from_groups(values):
    moved = jnp.moveaxis(values, 0, -3)
    return moved.reshape(moved.shape[:-3] + (-1,))


def attend(group_in, column_ok, score_scale):
    query_g, key_g, value_g, outgrad_g = group_in
    scores = (
        jnp.einsum("qhd,khd->hqk", query_g, key_g, preferred_element_type=jnp.float32) * score_scale
    )
    scores = jnp.where(column_ok[None, None, :], scores, -1e30)
    expos = jnp.exp(scores)
    row_sum = jnp.sum(expos, axis=2)
    probs = expos / row_sum[:, :, None]
    probs_b = probs.astype(jnp.bfloat16)
    attended = jnp.einsum(
        "hqk,khd->qhd", probs_b, value_g, preferred_element_type=jnp.float32
    ).astype(jnp.bfloat16)
    delta = jnp.einsum("qhd,qhd->hq", outgrad_g, attended, preferred_element_type=jnp.float32)
    prob_grad = jnp.einsum("qhd,khd->hqk", outgrad_g, value_g, preferred_element_type=jnp.float32)
    score_grad = (probs * (prob_grad - delta[:, :, None]) * score_scale).astype(jnp.bfloat16)
    query_grad = jnp.einsum(
        "hqk,khd->qhd", score_grad, key_g, preferred_element_type=jnp.float32
    ).astype(jnp.bfloat16)
    key_part = jnp.einsum(
        "hqk,qhd->khd", score_grad, query_g, preferred_element_type=jnp.float32
    ).astype(jnp.bfloat16)
    value_part = jnp.einsum(
        "hqk,qhd->khd", probs_b, outgrad_g, preferred_element_type=jnp.float32
    ).astype(jnp.bfloat16)
    return (attended, query_grad, key_part, value_part, row_sum, delta)


def per_device(layer_inputs, final_cot, attn_weights, norm_gain, pair_list, pair_count):
    segments = lax.axis_size("segment")
    my_segment = lax.axis_index("segment")
    my_block = lax.axis_index("blk")
    block_count = lax.axis_size("blk")
    walkers = layer_inputs.shape[1]
    block_rows = layer_inputs.shape[2]
    feat_width = layer_inputs.shape[3]
    head_size = feat_width // HEADS
    score_scale = head_size ** (-0.5)
    slot_total = pair_list.shape[1]
    weights = attn_weights[0]
    gain_row = norm_gain[0]
    own_inputs = layer_inputs[0]
    my_list = lax.dynamic_index_in_dim(pair_list, my_block, 0, keepdims=False)
    my_count = lax.dynamic_index_in_dim(pair_count, my_block, 0, keepdims=False)
    slot_ok = jnp.arange(slot_total) < my_count
    column_ok = jnp.repeat(slot_ok, block_rows)
    tick_count = walkers + segments - 1

    def one_tick(tick_no, state_all):
        incoming, cot_store, grad_sum, gain_sum = state_all
        walker_no = tick_no - (segments - 1 - my_segment)
        is_live = (walker_no >= 0) & (walker_no < walkers)
        walker_idx = jnp.clip(walker_no, 0, walkers - 1)
        inputs = lax.dynamic_index_in_dim(own_inputs, walker_idx, 0, keepdims=False)
        last_cot = lax.dynamic_index_in_dim(final_cot, walker_idx, 0, keepdims=False)
        cotangent = jnp.where(my_segment == segments - 1, last_cot, incoming)
        unit_feat, inv_rms, normed = rms_parts(inputs, gain_row)
        queries = jnp.dot(normed, weights[0], preferred_element_type=jnp.float32).astype(
            jnp.bfloat16
        )
        out_grad = jnp.dot(cotangent, weights[3].T, preferred_element_type=jnp.float32).astype(
            jnp.bfloat16
        )
        all_normed = lax.all_gather(normed, "blk", axis=0, tiled=True)
        picked = all_normed.reshape(block_count, block_rows, feat_width)[my_list].reshape(
            -1, feat_width
        )
        keys_near = jnp.dot(picked, weights[1], preferred_element_type=jnp.float32).astype(
            jnp.bfloat16
        )
        values_near = jnp.dot(picked, weights[2], preferred_element_type=jnp.float32).astype(
            jnp.bfloat16
        )
        group_out = lax.map(
            partial(attend, column_ok=column_ok, score_scale=score_scale),
            (
                to_groups(queries, head_size),
                to_groups(keys_near, head_size),
                to_groups(values_near, head_size),
                to_groups(out_grad, head_size),
            ),
        )
        attended_g, query_grad_g, key_part_g, value_part_g, sum_g, delta_g = group_out
        attended = from_groups(attended_g)
        query_grad = from_groups(query_grad_g)
        stacked = jnp.concatenate([from_groups(key_part_g), from_groups(value_part_g)], axis=1)
        placed = jnp.zeros((block_count, block_rows, 2 * feat_width), jnp.float32)
        placed = placed.at[my_list].set(
            stacked.reshape(slot_total, block_rows, 2 * feat_width).astype(jnp.float32)
        )
        summed = lax.psum_scatter(
            placed.reshape(-1, 2 * feat_width).astype(jnp.bfloat16),
            "blk",
            scatter_dimension=0,
            tiled=True,
        ).astype(jnp.float32)
        key_grad = summed[:, :feat_width].astype(jnp.bfloat16)
        value_grad = summed[:, feat_width:].astype(jnp.bfloat16)
        normed_grad = (
            jnp.dot(query_grad, weights[0].T, preferred_element_type=jnp.float32)
            + jnp.dot(key_grad, weights[1].T, preferred_element_type=jnp.float32)
            + jnp.dot(value_grad, weights[2].T, preferred_element_type=jnp.float32)
        )
        gain_part = jnp.sum(normed_grad * unit_feat, axis=0)
        input_grad = (
            cotangent.astype(jnp.float32) + norm_back(normed_grad, unit_feat, inv_rms, gain_row)
        ).astype(jnp.bfloat16)
        grad_part = jnp.stack(
            [
                jnp.dot(normed.T, query_grad, preferred_element_type=jnp.float32),
                jnp.dot(normed.T, key_grad, preferred_element_type=jnp.float32),
                jnp.dot(normed.T, value_grad, preferred_element_type=jnp.float32),
                jnp.dot(attended.T, cotangent, preferred_element_type=jnp.float32),
            ]
        )
        grad_sum = grad_sum + jnp.where(is_live, grad_part, 0.0)
        gain_sum = gain_sum + jnp.where(is_live, gain_part, 0.0)
        current = lax.dynamic_index_in_dim(cot_store, walker_idx, 0, keepdims=False)
        cot_store = lax.dynamic_update_index_in_dim(
            cot_store, jnp.where(is_live, input_grad, current), walker_idx, 0
        )
        incoming = shifted(input_grad, "segment", -1)
        return (incoming, cot_store, grad_sum, gain_sum)

    start_state = (
        jnp.zeros((block_rows, feat_width), jnp.bfloat16),
        jnp.zeros_like(own_inputs),
        jnp.zeros((4, feat_width, feat_width), jnp.float32),
        jnp.zeros((feat_width,), jnp.float32),
    )
    final_state = lax.fori_loop(0, tick_count, one_tick, start_state)
    grad_total, gain_total = (
        lax.psum(final_state[2].astype(jnp.bfloat16), "blk").astype(jnp.float32),
        lax.psum(final_state[3].astype(jnp.bfloat16), "blk").astype(jnp.float32),
    )
    return (final_state[1][None], grad_total[None], gain_total[None])


def solution(mesh):
    return jax.shard_map(
        per_device,
        mesh=mesh,
        in_specs=(
            P("segment", None, "blk", None),
            P(None, "blk", None),
            P("segment", None, None, None),
            P("segment", None),
            P(),
            P(),
        ),
        out_specs=(
            P("segment", None, "blk", None),
            P("segment", None, None, None),
            P("segment", None),
        ),
        check_vma=False,
    )
```

profile of v0, /device:TPU:0, one launch (start us, length us, event | category | flops | bytes accessed | tf_op | source)
XLA Modules:
  0.0 796.0 jit_solution(654499280079027165)
XLA Ops:
  10.9 718.5 %while.76 = (s32[]{:T(128)}, bf16[128,256]{1,0:T(8,128)(2,1)S(1)}, bf16[6,128,256]{2,1,0:T(8,128)(2,1)}, f32[4,256,256]{2,1,0:T(8,128)}, f32[256]{0:T(256)}, /*i...) while((s32[]{:T(128)}, bf16[128,256]{1,0:T(8,128)(2,1)S(1)}, ...), condition=%wide.region_9.10_spmd.clone, body=%wide.region_0.9_spmd.clone.sunk | while | flops 352080000 | bytes 50344628 | solution.py:176
  13.0 11.3 %all_gather.11 = bf16[1024,256]{1,0:T(8,128)(2,1)S(1)} all-gather(bf16[128,256]{1,0:T(8,128)(2,1)S(1)} %fusion.178), channel_id=1, replica_groups=mesh['segment'=4,'blk'=8] {'blk'}, dimensions={0}, use_global_device_ids=true | all-gather | bytes 589824 | tf_op jit(solution)/shard_map/while/body/eval_jaxpr/all_gather | solution.py:109
  29.7 14.2 %while.77 = (s32[]{:T(128)}, bf16[4,128,4,16]{1,3,2,0:T(8,128)(2,1)}, bf16[4,128,4,16]{1,3,2,0:T(8,128)(2,1)}, bf16[4,512,4,16]{1,3,2,0:T(8,128)(2,1)S(1)}, bf16...) while((s32[]{:T(128)}, ...), condition=%wide.region_4.4_spmd, body=%wide.region_2.3_spmd.sunk | while | flops 62245376 | bytes 9547889 | solution.py:119
  48.4 34.9 %reduce-scatter.2.cloned.1.call-done = bf16[128,512]{1,0:T(8,128)(2,1)} async-done(((bf16[1024,512]{1,0:T(8,128)(2,1)}), bf16[128,512]{1,0:T(8,128)(2,1)}) %reduce-scatter.2.cloned.1.call-update) | async-done | bytes 131088 | tf_op jit(solution)/shard_map/while/body/eval_jaxpr/reduce_scatter | solution.py:136
  86.3 1.4 collective-permute-start
  90.3 2.3 collective-permute-done
  94.7 9.8 %all_gather.11 = bf16[1024,256]{1,0:T(8,128)(2,1)S(1)} all-gather(bf16[128,256]{1,0:T(8,128)(2,1)S(1)} %fusion.178), channel_id=1, replica_groups=mesh['segment'=4,'blk'=8] {'blk'}, dimensions={0}, use_global_device_ids=true | all-gather | bytes 589824 | tf_op jit(solution)/shard_map/while/body/eval_jaxpr/all_gather | solution.py:109
  109.9 14.2 %while.77 = (s32[]{:T(128)}, bf16[4,128,4,16]{1,3,2,0:T(8,128)(2,1)}, bf16[4,128,4,16]{1,3,2,0:T(8,128)(2,1)}, bf16[4,512,4,16]{1,3,2,0:T(8,128)(2,1)S(1)}, bf16...) while((s32[]{:T(128)}, ...), condition=%wide.region_4.4_spmd, body=%wide.region_2.3_spmd.sunk | while | flops 62245376 | bytes 9547889 | solution.py:119
  128.6 34.3 %reduce-scatter.2.cloned.1.call-done = bf16[128,512]{1,0:T(8,128)(2,1)} async-done(((bf16[1024,512]{1,0:T(8,128)(2,1)}), bf16[128,512]{1,0:T(8,128)(2,1)}) %reduce-scatter.2.cloned.1.call-update) | async-done | bytes 131088 | tf_op jit(solution)/shard_map/while/body/eval_jaxpr/reduce_scatter | solution.py:136
  165.9 1.4 collective-permute-start
  169.9 2.3 collective-permute-done
  174.3 9.8 %all_gather.11 = bf16[1024,256]{1,0:T(8,128)(2,1)S(1)} all-gather(bf16[128,256]{1,0:T(8,128)(2,1)S(1)} %fusion.178), channel_id=1, replica_groups=mesh['segment'=4,'blk'=8] {'blk'}, dimensions={0}, use_global_device_ids=true | all-gather | bytes 589824 | tf_op jit(solution)/shard_map/while/body/eval_jaxpr/all_gather | solution.py:109
  189.5 14.2 %while.77 = (s32[]{:T(128)}, bf16[4,128,4,16]{1,3,2,0:T(8,128)(2,1)}, bf16[4,128,4,16]{1,3,2,0:T(8,128)(2,1)}, bf16[4,512,4,16]{1,3,2,0:T(8,128)(2,1)S(1)}, bf16...) while((s32[]{:T(128)}, ...), condition=%wide.region_4.4_spmd, body=%wide.region_2.3_spmd.sunk | while | flops 62245376 | bytes 9547889 | solution.py:119
  208.2 34.3 %reduce-scatter.2.cloned.1.call-done = bf16[128,512]{1,0:T(8,128)(2,1)} async-done(((bf16[1024,512]{1,0:T(8,128)(2,1)}), bf16[128,512]{1,0:T(8,128)(2,1)}) %reduce-scatter.2.cloned.1.call-update) | async-done | bytes 131088 | tf_op jit(solution)/shard_map/while/body/eval_jaxpr/reduce_scatter | solution.py:136
  245.5 1.4 collective-permute-start
  249.5 2.3 collective-permute-done
  253.9 9.8 %all_gather.11 = bf16[1024,256]{1,0:T(8,128)(2,1)S(1)} all-gather(bf16[128,256]{1,0:T(8,128)(2,1)S(1)} %fusion.178), channel_id=1, replica_groups=mesh['segment'=4,'blk'=8] {'blk'}, dimensions={0}, use_global_device_ids=true | all-gather | bytes 589824 | tf_op jit(solution)/shard_map/while/body/eval_jaxpr/all_gather | solution.py:109
  269.1 14.2 %while.77 = (s32[]{:T(128)}, bf16[4,128,4,16]{1,3,2,0:T(8,128)(2,1)}, bf16[4,128,4,16]{1,3,2,0:T(8,128)(2,1)}, bf16[4,512,4,16]{1,3,2,0:T(8,128)(2,1)S(1)}, bf16...) while((s32[]{:T(128)}, ...), condition=%wide.region_4.4_spmd, body=%wide.region_2.3_spmd.sunk | while | flops 62245376 | bytes 9547889 | solution.py:119
  287.8 34.3 %reduce-scatter.2.cloned.1.call-done = bf16[128,512]{1,0:T(8,128)(2,1)} async-done(((bf16[1024,512]{1,0:T(8,128)(2,1)}), bf16[128,512]{1,0:T(8,128)(2,1)}) %reduce-scatter.2.cloned.1.call-update) | async-done | bytes 131088 | tf_op jit(solution)/shard_map/while/body/eval_jaxpr/reduce_scatter | solution.py:136
  325.1 1.4 collective-permute-start
  329.1 2.3 collective-permute-done
  333.5 9.8 %all_gather.11 = bf16[1024,256]{1,0:T(8,128)(2,1)S(1)} all-gather(bf16[128,256]{1,0:T(8,128)(2,1)S(1)} %fusion.178), channel_id=1, replica_groups=mesh['segment'=4,'blk'=8] {'blk'}, dimensions={0}, use_global_device_ids=true | all-gather | bytes 589824 | tf_op jit(solution)/shard_map/while/body/eval_jaxpr/all_gather | solution.py:109
  348.7 14.2 %while.77 = (s32[]{:T(128)}, bf16[4,128,4,16]{1,3,2,0:T(8,128)(2,1)}, bf16[4,128,4,16]{1,3,2,0:T(8,128)(2,1)}, bf16[4,512,4,16]{1,3,2,0:T(8,128)(2,1)S(1)}, bf16...) while((s32[]{:T(128)}, ...), condition=%wide.region_4.4_spmd, body=%wide.region_2.3_spmd.sunk | while | flops 62245376 | bytes 9547889 | solution.py:119
  367.4 34.3 %reduce-scatter.2.cloned.1.call-done = bf16[128,512]{1,0:T(8,128)(2,1)} async-done(((bf16[1024,512]{1,0:T(8,128)(2,1)}), bf16[128,512]{1,0:T(8,128)(2,1)}) %reduce-scatter.2.cloned.1.call-update) | async-done | bytes 131088 | tf_op jit(solution)/shard_map/while/body/eval_jaxpr/reduce_scatter | solution.py:136
  404.7 1.4 collective-permute-start
  408.7 2.3 collective-permute-done
  413.1 9.8 %all_gather.11 = bf16[1024,256]{1,0:T(8,128)(2,1)S(1)} all-gather(bf16[128,256]{1,0:T(8,128)(2,1)S(1)} %fusion.178), channel_id=1, replica_groups=mesh['segment'=4,'blk'=8] {'blk'}, dimensions={0}, use_global_device_ids=true | all-gather | bytes 589824 | tf_op jit(solution)/shard_map/while/body/eval_jaxpr/all_gather | solution.py:109
  428.3 14.2 %while.77 = (s32[]{:T(128)}, bf16[4,128,4,16]{1,3,2,0:T(8,128)(2,1)}, bf16[4,128,4,16]{1,3,2,0:T(8,128)(2,1)}, bf16[4,512,4,16]{1,3,2,0:T(8,128)(2,1)S(1)}, bf16...) while((s32[]{:T(128)}, ...), condition=%wide.region_4.4_spmd, body=%wide.region_2.3_spmd.sunk | while | flops 62245376 | bytes 9547889 | solution.py:119
  447.0 34.3 %reduce-scatter.2.cloned.1.call-done = bf16[128,512]{1,0:T(8,128)(2,1)} async-done(((bf16[1024,512]{1,0:T(8,128)(2,1)}), bf16[128,512]{1,0:T(8,128)(2,1)}) %reduce-scatter.2.cloned.1.call-update) | async-done | bytes 131088 | tf_op jit(solution)/shard_map/while/body/eval_jaxpr/reduce_scatter | solution.py:136
  484.3 1.4 collective-permute-start
  488.3 2.3 collective-permute-done
  492.7 9.8 %all_gather.11 = bf16[1024,256]{1,0:T(8,128)(2,1)S(1)} all-gather(bf16[128,256]{1,0:T(8,128)(2,1)S(1)} %fusion.178), channel_id=1, replica_groups=mesh['segment'=4,'blk'=8] {'blk'}, dimensions={0}, use_global_device_ids=true | all-gather | bytes 589824 | tf_op jit(solution)/shard_map/while/body/eval_jaxpr/all_gather | solution.py:109
  507.9 14.2 %while.77 = (s32[]{:T(128)}, bf16[4,128,4,16]{1,3,2,0:T(8,128)(2,1)}, bf16[4,128,4,16]{1,3,2,0:T(8,128)(2,1)}, bf16[4,512,4,16]{1,3,2,0:T(8,128)(2,1)S(1)}, bf16...) while((s32[]{:T(128)}, ...), condition=%wide.region_4.4_spmd, body=%wide.region_2.3_spmd.sunk | while | flops 62245376 | bytes 9547889 | solution.py:119
  526.6 34.3 %reduce-scatter.2.cloned.1.call-done = bf16[128,512]{1,0:T(8,128)(2,1)} async-done(((bf16[1024,512]{1,0:T(8,128)(2,1)}), bf16[128,512]{1,0:T(8,128)(2,1)}) %reduce-scatter.2.cloned.1.call-update) | async-done | bytes 131088 | tf_op jit(solution)/shard_map/while/body/eval_jaxpr/reduce_scatter | solution.py:136
  563.9 1.4 collective-permute-start
  567.9 2.3 collective-permute-done
  572.3 9.8 %all_gather.11 = bf16[1024,256]{1,0:T(8,128)(2,1)S(1)} all-gather(bf16[128,256]{1,0:T(8,128)(2,1)S(1)} %fusion.178), channel_id=1, replica_groups=mesh['segment'=4,'blk'=8] {'blk'}, dimensions={0}, use_global_device_ids=true | all-gather | bytes 589824 | tf_op jit(solution)/shard_map/while/body/eval_jaxpr/all_gather | solution.py:109
  587.5 14.2 %while.77 = (s32[]{:T(128)}, bf16[4,128,4,16]{1,3,2,0:T(8,128)(2,1)}, bf16[4,128,4,16]{1,3,2,0:T(8,128)(2,1)}, bf16[4,512,4,16]{1,3,2,0:T(8,128)(2,1)S(1)}, bf16...) while((s32[]{:T(128)}, ...), condition=%wide.region_4.4_spmd, body=%wide.region_2.3_spmd.sunk | while | flops 62245376 | bytes 9547889 | solution.py:119
  606.2 34.3 %reduce-scatter.2.cloned.1.call-done = bf16[128,512]{1,0:T(8,128)(2,1)} async-done(((bf16[1024,512]{1,0:T(8,128)(2,1)}), bf16[128,512]{1,0:T(8,128)(2,1)}) %reduce-scatter.2.cloned.1.call-update) | async-done | bytes 131088 | tf_op jit(solution)/shard_map/while/body/eval_jaxpr/reduce_scatter | solution.py:136
  647.5 2.3 collective-permute-done
  651.9 9.8 %all_gather.11 = bf16[1024,256]{1,0:T(8,128)(2,1)S(1)} all-gather(bf16[128,256]{1,0:T(8,128)(2,1)S(1)} %fusion.178), channel_id=1, replica_groups=mesh['segment'=4,'blk'=8] {'blk'}, dimensions={0}, use_global_device_ids=true | all-gather | bytes 589824 | tf_op jit(solution)/shard_map/while/body/eval_jaxpr/all_gather | solution.py:109
  667.1 14.2 %while.77 = (s32[]{:T(128)}, bf16[4,128,4,16]{1,3,2,0:T(8,128)(2,1)}, bf16[4,128,4,16]{1,3,2,0:T(8,128)(2,1)}, bf16[4,512,4,16]{1,3,2,0:T(8,128)(2,1)S(1)}, bf16...) while((s32[]{:T(128)}, ...), condition=%wide.region_4.4_spmd, body=%wide.region_2.3_spmd.sunk | while | flops 62245376 | bytes 9547889 | solution.py:119
  685.8 34.3 %reduce-scatter.2.cloned.1.call-done = bf16[128,512]{1,0:T(8,128)(2,1)} async-done(((bf16[1024,512]{1,0:T(8,128)(2,1)}), bf16[128,512]{1,0:T(8,128)(2,1)}) %reduce-scatter.2.cloned.1.call-update) | async-done | bytes 131088 | tf_op jit(solution)/shard_map/while/body/eval_jaxpr/reduce_scatter | solution.py:136
  727.1 2.3 collective-permute-done
  729.5 2.1 convert_bitcast_fusion.1
  731.6 11.9 %psum.15 = bf16[1,256]{1,0:T(2,128)(2,1)S(1)} all-reduce(bf16[1,256]{1,0:T(2,128)(2,1)S(1)} %broadcast_in_dim.108), channel_id=1, replica_groups=mesh['segment'=4,'blk'=8] {'blk'}, use_global_device_ids=true, to_apply=%region_11.12 | all-reduce | flops 256 | bytes 1024 | tf_op jit(solution)/shard_map/psum | solution.py:179
  744.1 42.7 %all-reduce.2.cloned.1.call-done = bf16[1,4,256,256]{3,2,1,0:T(8,128)(2,1)} async-done(((bf16[1,4,256,256]{3,2,1,0:T(8,128)(2,1)}), bf16[1,4,256,256]{3,2,1,0:T(8,128)(2,1)}) %all-reduce.2.cloned.1.call-update) | async-done | bytes 524304 | tf_op jit(solution)/shard_map/psum | solution.py:178
  786.8 2.1 broadcast_in_dim.107
  (918 shorter events, 287.3 us)
Async XLA Ops:
  10.9 17.4 %copy-start.12 = (s32[4]{0:T(128)}, s32[4]{0:T(128)S(1)}, u32[]{:S(2)}) copy-start(s32[4]{0:T(128)S(1)} %get-tuple-element.710) | copy-start | bytes 52 | tf_op jit(solution)/shard_map/while
  10.9 18.8 %copy-start.14 = (pred[4]{0:T(512)(128)(4,1)}, pred[4]{0:T(512)(128)(4,1)S(1)}, u32[]{:S(2)}) copy-start(pred[4]{0:T(512)(128)(4,1)S(1)} %get-tuple-element.711) | copy-start | bytes 16 | tf_op jit(solution)/shard_map/while
  10.9 16.3 %copy-start.3 = (bf16[4,256,256]{2,1,0:T(8,128)(2,1)S(1)}, bf16[4,256,256]{2,1,0:T(8,128)(2,1)}, u32[]{:S(2)}) copy-start(bf16[4,256,256]{2,1,0:T(8,128)(2,1)} %get-tuple-element.709) | copy-start | bytes 1572868 | tf_op jit(solution)/shard_map/while
  10.9 16.3 %copy-start.8 = (f32[1,256]{1,0:T(1,128)S(1)}, f32[1,256]{1,0:T(1,128)}, u32[]{:S(2)}) copy-start(f32[1,256]{1,0:T(1,128)} %get-tuple-element.708) | copy-start | bytes 3076 | tf_op jit(solution)/shard_map/while
  11.0 72.4 %reduce-scatter.2.cloned.1.call-start = ((), (), s32[]{:S(2)}) async-start(), calls=%async_computation.2 | async-start | bytes 1179648 | tf_op jit(solution)/shard_map/while/body/eval_jaxpr/reduce_scatter | solution.py:136
  46.8 43.1 %copy-start.1 = (f32[4,256,256]{2,1,0:T(8,128)S(1)}, f32[4,256,256]{2,1,0:T(8,128)}, u32[]{:S(2)}) copy-start(f32[4,256,256]{2,1,0:T(8,128)} %get-tuple-element.683) | copy-start | bytes 3145732 | tf_op jit(solution)/shard_map/while
  86.3 6.3 collective-permute-start
  92.6 15.9 %copy-start.12 = (s32[4]{0:T(128)}, s32[4]{0:T(128)S(1)}, u32[]{:S(2)}) copy-start(s32[4]{0:T(128)S(1)} %get-tuple-element.710) | copy-start | bytes 52 | tf_op jit(solution)/shard_map/while
  92.6 17.3 %copy-start.14 = (pred[4]{0:T(512)(128)(4,1)}, pred[4]{0:T(512)(128)(4,1)S(1)}, u32[]{:S(2)}) copy-start(pred[4]{0:T(512)(128)(4,1)S(1)} %get-tuple-element.711) | copy-start | bytes 16 | tf_op jit(solution)/shard_map/while
  92.7 70.3 %reduce-scatter.2.cloned.1.call-start = ((), (), s32[]{:S(2)}) async-start(), calls=%async_computation.2 | async-start | bytes 1179648 | tf_op jit(solution)/shard_map/while/body/eval_jaxpr/reduce_scatter | solution.py:136
  127.0 42.5 %copy-start.1 = (f32[4,256,256]{2,1,0:T(8,128)S(1)}, f32[4,256,256]{2,1,0:T(8,128)}, u32[]{:S(2)}) copy-start(f32[4,256,256]{2,1,0:T(8,128)} %get-tuple-element.683) | copy-start | bytes 3145732 | tf_op jit(solution)/shard_map/while
  165.9 6.3 collective-permute-start
  172.2 15.9 %copy-start.12 = (s32[4]{0:T(128)}, s32[4]{0:T(128)S(1)}, u32[]{:S(2)}) copy-start(s32[4]{0:T(128)S(1)} %get-tuple-element.710) | copy-start | bytes 52 | tf_op jit(solution)/shard_map/while
  172.2 17.3 %copy-start.14 = (pred[4]{0:T(512)(128)(4,1)}, pred[4]{0:T(512)(128)(4,1)S(1)}, u32[]{:S(2)}) copy-start(pred[4]{0:T(512)(128)(4,1)S(1)} %get-tuple-element.711) | copy-start | bytes 16 | tf_op jit(solution)/shard_map/while
  172.3 70.3 %reduce-scatter.2.cloned.1.call-start = ((), (), s32[]{:S(2)}) async-start(), calls=%async_computation.2 | async-start | bytes 1179648 | tf_op jit(solution)/shard_map/while/body/eval_jaxpr/reduce_scatter | solution.py:136
  206.6 42.5 %copy-start.1 = (f32[4,256,256]{2,1,0:T(8,128)S(1)}, f32[4,256,256]{2,1,0:T(8,128)}, u32[]{:S(2)}) copy-start(f32[4,256,256]{2,1,0:T(8,128)} %get-tuple-element.683) | copy-start | bytes 3145732 | tf_op jit(solution)/shard_map/while
  245.5 6.3 collective-permute-start
  251.8 15.8 %copy-start.12 = (s32[4]{0:T(128)}, s32[4]{0:T(128)S(1)}, u32[]{:S(2)}) copy-start(s32[4]{0:T(128)S(1)} %get-tuple-element.710) | copy-start | bytes 52 | tf_op jit(solution)/shard_map/while
  251.9 17.3 %copy-start.14 = (pred[4]{0:T(512)(128)(4,1)}, pred[4]{0:T(512)(128)(4,1)S(1)}, u32[]{:S(2)}) copy-start(pred[4]{0:T(512)(128)(4,1)S(1)} %get-tuple-element.711) | copy-start | bytes 16 | tf_op jit(solution)/shard_map/while
  251.9 70.2 %reduce-scatter.2.cloned.1.call-start = ((), (), s32[]{:S(2)}) async-start(), calls=%async_computation.2 | async-start | bytes 1179648 | tf_op jit(solution)/shard_map/while/body/eval_jaxpr/reduce_scatter | solution.py:136
  286.2 42.5 %copy-start.1 = (f32[4,256,256]{2,1,0:T(8,128)S(1)}, f32[4,256,256]{2,1,0:T(8,128)}, u32[]{:S(2)}) copy-start(f32[4,256,256]{2,1,0:T(8,128)} %get-tuple-element.683) | copy-start | bytes 3145732 | tf_op jit(solution)/shard_map/while
  325.1 6.3 collective-permute-start
  331.4 15.9 %copy-start.12 = (s32[4]{0:T(128)}, s32[4]{0:T(128)S(1)}, u32[]{:S(2)}) copy-start(s32[4]{0:T(128)S(1)} %get-tuple-element.710) | copy-start | bytes 52 | tf_op jit(solution)/shard_map/while
  331.4 17.3 %copy-start.14 = (pred[4]{0:T(512)(128)(4,1)}, pred[4]{0:T(512)(128)(4,1)S(1)}, u32[]{:S(2)}) copy-start(pred[4]{0:T(512)(128)(4,1)S(1)} %get-tuple-element.711) | copy-start | bytes 16 | tf_op jit(solution)/shard_map/while
  331.5 70.2 %reduce-scatter.2.cloned.1.call-start = ((), (), s32[]{:S(2)}) async-start(), calls=%async_computation.2 | async-start | bytes 1179648 | tf_op jit(solution)/shard_map/while/body/eval_jaxpr/reduce_scatter | solution.py:136
  365.8 42.5 %copy-start.1 = (f32[4,256,256]{2,1,0:T(8,128)S(1)}, f32[4,256,256]{2,1,0:T(8,128)}, u32[]{:S(2)}) copy-start(f32[4,256,256]{2,1,0:T(8,128)} %get-tuple-element.683) | copy-start | bytes 3145732 | tf_op jit(solution)/shard_map/while
  404.7 6.3 collective-permute-start
  411.0 15.9 %copy-start.12 = (s32[4]{0:T(128)}, s32[4]{0:T(128)S(1)}, u32[]{:S(2)}) copy-start(s32[4]{0:T(128)S(1)} %get-tuple-element.710) | copy-start | bytes 52 | tf_op jit(solution)/shard_map/while
  411.0 17.3 %copy-start.14 = (pred[4]{0:T(512)(128)(4,1)}, pred[4]{0:T(512)(128)(4,1)S(1)}, u32[]{:S(2)}) copy-start(pred[4]{0:T(512)(128)(4,1)S(1)} %get-tuple-element.711) | copy-start | bytes 16 | tf_op jit(solution)/shard_map/while
  411.1 70.2 %reduce-scatter.2.cloned.1.call-start = ((), (), s32[]{:S(2)}) async-start(), calls=%async_computation.2 | async-start | bytes 1179648 | tf_op jit(solution)/shard_map/while/body/eval_jaxpr/reduce_scatter | solution.py:136
  445.4 42.5 %copy-start.1 = (f32[4,256,256]{2,1,0:T(8,128)S(1)}, f32[4,256,256]{2,1,0:T(8,128)}, u32[]{:S(2)}) copy-start(f32[4,256,256]{2,1,0:T(8,128)} %get-tuple-element.683) | copy-start | bytes 3145732 | tf_op jit(solution)/shard_map/while
  484.3 6.3 collective-permute-start
  490.6 15.9 %copy-start.12 = (s32[4]{0:T(128)}, s32[4]{0:T(128)S(1)}, u32[]{:S(2)}) copy-start(s32[4]{0:T(128)S(1)} %get-tuple-element.710) | copy-start | bytes 52 | tf_op jit(solution)/shard_map/while
  490.6 17.3 %copy-start.14 = (pred[4]{0:T(512)(128)(4,1)}, pred[4]{0:T(512)(128)(4,1)S(1)}, u32[]{:S(2)}) copy-start(pred[4]{0:T(512)(128)(4,1)S(1)} %get-tuple-element.711) | copy-start | bytes 16 | tf_op jit(solution)/shard_map/while
  490.7 70.3 %reduce-scatter.2.cloned.1.call-start = ((), (), s32[]{:S(2)}) async-start(), calls=%async_computation.2 | async-start | bytes 1179648 | tf_op jit(solution)/shard_map/while/body/eval_jaxpr/reduce_scatter | solution.py:136
  525.0 42.5 %copy-start.1 = (f32[4,256,256]{2,1,0:T(8,128)S(1)}, f32[4,256,256]{2,1,0:T(8,128)}, u32[]{:S(2)}) copy-start(f32[4,256,256]{2,1,0:T(8,128)} %get-tuple-element.683) | copy-start | bytes 3145732 | tf_op jit(solution)/shard_map/while
  563.9 6.3 collective-permute-start
  570.2 15.8 %copy-start.12 = (s32[4]{0:T(128)}, s32[4]{0:T(128)S(1)}, u32[]{:S(2)}) copy-start(s32[4]{0:T(128)S(1)} %get-tuple-element.710) | copy-start | bytes 52 | tf_op jit(solution)/shard_map/while
  570.3 17.3 %copy-start.14 = (pred[4]{0:T(512)(128)(4,1)}, pred[4]{0:T(512)(128)(4,1)S(1)}, u32[]{:S(2)}) copy-start(pred[4]{0:T(512)(128)(4,1)S(1)} %get-tuple-element.711) | copy-start | bytes 16 | tf_op jit(solution)/shard_map/while
  570.3 70.2 %reduce-scatter.2.cloned.1.call-start = ((), (), s32[]{:S(2)}) async-start(), calls=%async_computation.2 | async-start | bytes 1179648 | tf_op jit(solution)/shard_map/while/body/eval_jaxpr/reduce_scatter | solution.py:136
  604.6 42.5 %copy-start.1 = (f32[4,256,256]{2,1,0:T(8,128)S(1)}, f32[4,256,256]{2,1,0:T(8,128)}, u32[]{:S(2)}) copy-start(f32[4,256,256]{2,1,0:T(8,128)} %get-tuple-element.683) | copy-start | bytes 3145732 | tf_op jit(solution)/shard_map/while
  643.5 6.3 collective-permute-start
  649.8 15.9 %copy-start.12 = (s32[4]{0:T(128)}, s32[4]{0:T(128)S(1)}, u32[]{:S(2)}) copy-start(s32[4]{0:T(128)S(1)} %get-tuple-element.710) | copy-start | bytes 52 | tf_op jit(solution)/shard_map/while
  649.8 17.3 %copy-start.14 = (pred[4]{0:T(512)(128)(4,1)}, pred[4]{0:T(512)(128)(4,1)S(1)}, u32[]{:S(2)}) copy-start(pred[4]{0:T(512)(128)(4,1)S(1)} %get-tuple-element.711) | copy-start | bytes 16 | tf_op jit(solution)/shard_map/while
  649.9 70.2 %reduce-scatter.2.cloned.1.call-start = ((), (), s32[]{:S(2)}) async-start(), calls=%async_computation.2 | async-start | bytes 1179648 | tf_op jit(solution)/shard_map/while/body/eval_jaxpr/reduce_scatter | solution.py:136
  684.2 42.5 %copy-start.1 = (f32[4,256,256]{2,1,0:T(8,128)S(1)}, f32[4,256,256]{2,1,0:T(8,128)}, u32[]{:S(2)}) copy-start(f32[4,256,256]{2,1,0:T(8,128)} %get-tuple-element.683) | copy-start | bytes 3145732 | tf_op jit(solution)/shard_map/while
  723.1 6.3 collective-permute-start
  729.4 57.3 %all-reduce.2.cloned.1.call-start = ((), (), s32[]{:S(2)}) async-start(), calls=%async_computation.1 | async-start | bytes 1048576 | tf_op jit(solution)/shard_map/psum | solution.py:178
  (99 other events, 529.1 us)
Sparse Core Ops, SparseCore 0:
  46.9 36.3 reduce-scatter.1
  127.1 35.7 reduce-scatter.1
  206.7 35.7 reduce-scatter.1
  286.3 35.7 reduce-scatter.1
  365.9 35.7 reduce-scatter.1
  445.5 35.7 reduce-scatter.1
  525.1 35.7 reduce-scatter.1
  604.7 35.7 reduce-scatter.1
  684.3 35.7 reduce-scatter.1
Sparse Core Ops, SparseCore 1:
  733.0 53.7 all-reduce.1
where the time goes:
time: 800 us; the launch traced here: 796 us
  waiting for transfers between devices  373 us (47%)
  matrix products  202 us (25%)
  blocking collectives  101 us (13%)
  other arithmetic  53.2 us (7%)
  local copies, waits for them, and re-layouts  33 us (4%)
  between operations  15.2 us (2%)
  starting transfers between devices  13.1 us (2%)
    reduce_scatter x9, waiting for transfers between devices, one_tick(): lax.psum_scatter(placed.reshape(-1, 2 * feat_width).astype(jnp.bfloat16),...  309 us
    all_gather x9, blocking collectives, one_tick(): all_normed = lax.all_gather(normed, 'blk', axis=0, tiled=True)  89.5 us
    psum x1, waiting for transfers between devices, per_device(): lax.psum(final_state[2].astype(jnp.bfloat16), 'blk').astype(jnp.float32)  42.7 us
    dot_general x36, matrix products, attend(): jnp.einsum('hqk,khd->qhd', probs_b, value_g, preferred_element_type=jnp.f...  34.2 us
    dot_general x36, matrix products, attend(): jnp.einsum('hqk,khd->qhd', score_grad, key_g, preferred_element_type=jnp....  31.5 us
    ppermute x9, waiting for transfers between devices, shifted(): lax.ppermute(value, axis, [(source, source + steps) for source in range(i...  21 us
    div x36, matrix products, attend(): probs = expos / row_sum[:, :, None]  17.6 us
  transfers between devices with their start and end apart: 19, of which 19 were waited for; matrix products, arithmetic and copies ran while one was open for 5% of the time, Pallas kernels for 0%

commit v1 on v0

v1 whole, which is shorter than its diff:
```python
from functools import partial

import jax
import jax.numpy as jnp
from jax import lax
from jax.sharding import PartitionSpec as P

HEADS = 16
EPS = 1e-05
BF = jnp.bfloat16
F32 = jnp.float32


def mm(spec, *args):
    return jnp.einsum(spec, *args, preferred_element_type=F32)


def attend(one, heads, scale):
    q, k, v, out_grad, ok, masks = one
    rows = q.shape[0]
    near = k.shape[0]
    qm = (q[None] * masks).reshape(heads * rows, -1)
    om = (out_grad[None] * masks).reshape(heads * rows, -1)
    scores = mm("xd,kd->xk", qm, k) * scale
    expos = jnp.where(ok[None, :], jnp.exp(scores), 0.0)
    probs = expos / jnp.sum(expos, axis=1, keepdims=True)
    probs_b = probs.astype(BF)
    wide = masks.astype(F32)
    attended = jnp.sum(mm("xk,kd->xd", probs_b, v).reshape(heads, rows, -1) * wide, axis=0)
    attended = attended.astype(BF)
    delta = jnp.sum(
        om.reshape(heads, rows, -1).astype(F32) * attended[None].astype(F32), axis=2
    ).reshape(-1, 1)
    prob_grad = mm("xd,kd->xk", om, v)
    score_grad = (probs * (prob_grad - delta) * scale).astype(BF)
    query_grad = jnp.sum(mm("xk,kd->xd", score_grad, k).reshape(heads, rows, -1) * wide, axis=0)
    key_part = mm("xk,xd->kd", score_grad, qm).astype(BF)
    value_part = mm("xk,xd->kd", probs_b, om).astype(BF)
    return attended, query_grad.astype(BF), key_part, value_part


def per_device(layer_inputs, final_cot, attn_weights, norm_gain, pair_list, pair_count):
    segments = lax.axis_size("segment")
    seg = lax.axis_index("segment")
    blk = lax.axis_index("blk")
    block_count = lax.axis_size("blk")
    walkers, rows, width = layer_inputs.shape[1:]
    slots = pair_list.shape[1]
    head_size = width // HEADS
    half = blk % 2
    chip = blk // 2
    pieces = block_count // 2
    turns = walkers // 2
    own = 2 * rows
    w = attn_weights[0]
    gain = norm_gain

    places = ((pair_list // 2) ^ chip) * 2 + pair_list % 2
    my_lists = lax.dynamic_slice_in_dim(places, 2 * chip, 2, 0)
    my_counts = lax.dynamic_slice_in_dim(pair_count, 2 * chip, 2, 0)
    chosen = (my_lists[:, :, None] == jnp.arange(block_count)).astype(BF)
    ok = jnp.repeat(jnp.arange(slots)[None, :] < my_counts[:, None], rows, axis=1)
    masks = (jnp.arange(width)[None, :] // head_size == jnp.arange(HEADS)[:, None]).astype(BF)
    masks = masks[:, None, :]

    swap = [(i, i ^ 1) for i in range(block_count)]

    def to_walkers(values):
        split = values.reshape(turns, 2, rows, width)
        mine = lax.dynamic_index_in_dim(split, half, 1, keepdims=False)
        other = lax.ppermute(
            lax.dynamic_index_in_dim(split, 1 - half, 1, keepdims=False), "blk", swap
        )
        low = jnp.where(half == 0, mine, other)
        high = jnp.where(half == 0, other, mine)
        return jnp.concatenate([low, high], axis=1)

    x_own = to_walkers(layer_inputs[0])
    last_cot = to_walkers(final_cot)

    def xor_send(value, k):
        return lax.ppermute(value, "blk", [(i, i ^ (2 * k)) for i in range(block_count)])

    def one_walker(x, g):
        feats = x.astype(F32)
        inv = lax.rsqrt(jnp.mean(feats * feats, axis=-1, keepdims=True) + EPS)
        unit = feats * inv
        normed = (unit * gain).astype(BF)
        every = jnp.concatenate(
            [normed] + [xor_send(normed, k) for k in range(1, pieces)], axis=0
        )
        queries = mm("rd,de->re", normed, w[0]).astype(BF).reshape(2, rows, width)
        keys = mm("rd,de->re", every, w[1]).astype(BF).reshape(block_count, rows * width)
        values = mm("rd,de->re", every, w[2]).astype(BF).reshape(block_count, rows * width)
        keys = mm("acb,bx->acx", chosen, keys).astype(BF).reshape(2, slots * rows, width)
        values = mm("acb,bx->acx", chosen, values).astype(BF).reshape(2, slots * rows, width)
        out_grad = mm("rd,ed->re", g, w[3]).astype(BF).reshape(2, rows, width)
        parts = 4 if slots > 4 else 2
        one = partial(attend, heads=HEADS // parts, scale=head_size ** (-0.5))
        args = [jnp.repeat(arg, parts, axis=0) for arg in (queries, keys, values, out_grad, ok)]
        args.append(jnp.concatenate([masks.reshape(parts, HEADS // parts, 1, width)] * 2))
        summed = [
            jnp.sum(part.reshape((2, parts) + part.shape[1:]).astype(F32), axis=1).astype(BF)
            for part in lax.map(one, tuple(args))
        ]
        attended, query_grad, key_part, value_part = summed
        attended = attended.reshape(own, width)
        query_grad = query_grad.reshape(own, width)
        flat = (2, slots, rows * width)
        key_all = mm("acb,acx->bx", chosen, key_part.reshape(flat)).astype(BF)
        value_all = mm("acb,acx->bx", chosen, value_part.reshape(flat)).astype(BF)
        key_all = key_all.reshape(-1, width)
        value_all = value_all.reshape(-1, width)
        normed_grad = mm("re,de->rd", key_all, w[1]) + mm("re,de->rd", value_all, w[2])
        sends = normed_grad.astype(BF)
        total = normed_grad[:own] + mm("re,de->rd", query_grad, w[0])
        for k in range(1, pieces):
            total = total + xor_send(sends[k * own : (k + 1) * own], k).astype(F32)
        unit_grad = total * gain
        centre = jnp.mean(unit_grad * unit, axis=-1, keepdims=True)
        input_grad = (g.astype(F32) + inv * (unit_grad - unit * centre)).astype(BF)
        gain_part = jnp.sum(total * unit, axis=0, keepdims=True)
        grads = jnp.stack(
            [
                mm("rd,re->de", normed, query_grad),
                mm("rd,re->de", every, key_all),
                mm("rd,re->de", every, value_all),
                mm("rd,re->de", attended, g),
            ]
        )
        return input_grad, gain_part, grads

    incoming = jnp.zeros((own, width), BF)
    acc = jnp.zeros((4, width, width), F32)
    gain_acc = jnp.zeros((1, width), F32)
    cots = jnp.zeros((turns, own, width), BF)
    for tick in range(turns + segments - 1):
        turn = tick - (segments - 1 - seg)
        live = (turn >= 0) & (turn < turns)
        turn_at = jnp.clip(turn, 0, turns - 1)
        x = lax.dynamic_index_in_dim(x_own, turn_at, 0, keepdims=False)
        g = jnp.where(seg == segments - 1, last_cot[min(tick, turns - 1)], incoming)
        input_grad, gain_part, grads = one_walker(x, g)
        acc = acc + jnp.where(live, grads, 0.0)
        gain_acc = gain_acc + jnp.where(live, gain_part, 0.0)
        current = lax.dynamic_index_in_dim(cots, turn_at, 0, keepdims=False)
        cots = lax.dynamic_update_index_in_dim(
            cots, jnp.where(live, input_grad, current), turn_at, 0
        )
        if tick < turns + segments - 2:
            incoming = lax.ppermute(
                input_grad, "segment", [(i, (i - 1) % segments) for i in range(segments)]
            )

    halves = cots.reshape(turns, 2, rows, width)
    mine = lax.dynamic_index_in_dim(halves, half, 1, keepdims=False)
    other = lax.ppermute(
        lax.dynamic_index_in_dim(halves, 1 - half, 1, keepdims=False), "blk", swap
    )
    low = jnp.where(half == 0, mine, other)
    high = jnp.where(half == 0, other, mine)
    layer_cots = jnp.stack([low, high], axis=1).reshape(walkers, rows, width)

    flat = acc.astype(BF).reshape(block_count, -1, width)
    extra = jnp.broadcast_to(gain_acc.astype(BF)[None], (block_count, 16, width))
    got = lax.all_to_all(jnp.concatenate([flat, extra], axis=1), "blk", 0, 0)
    total = jnp.sum(got.astype(F32), axis=0)
    grads = lax.all_gather(total[:-16].astype(BF), "blk", axis=0, tiled=True)
    return (
        layer_cots[None],
        grads.astype(F32).reshape(1, 4, width, width),
        total[-16:-15],
    )


def solution(mesh):
    return jax.shard_map(
        per_device,
        mesh=mesh,
        in_specs=(
            P("segment", None, "blk", None),
            P(None, "blk", None),
            P("segment", None, None, None),
            P("segment", None),
            P(),
            P(),
        ),
        out_specs=(
            P("segment", None, "blk", None),
            P("segment", None, None, None),
            P("segment", None),
        ),
        check_vma=False,
    )
```

time: 800 us -> 507 us (0.63)
  waiting for transfers between devices: 373 us -> 22.3 us
  local copies, waits for them, and re-layouts: 33 us -> 148 us
  blocking collectives: 101 us -> 8.88 us
  starting transfers between devices: 13.1 us -> 58.9 us
  between operations: 15.2 us -> 3.42 us
    reduce_scatter x9 -> x0, waiting for transfers between devices: 309 us -> none  [one_tick(): lax.psum_scatter(placed.reshape(-1, 2 * feat_width).astype(jnp.bfloat16),...]
    all_gather x9 -> x1, blocking collectives: 89.5 us -> 8.88 us  [per_device(): grads = lax.all_gather(total[:-16].astype(BF), 'blk', axis=0, tiled=True)]
    psum x1 -> x0, waiting for transfers between devices: 42.7 us -> none  [per_device(): lax.psum(final_state[2].astype(jnp.bfloat16), 'blk').astype(jnp.float32)]
    ppermute x9 -> x44, starting transfers between devices: 12.7 us -> 55.3 us  [the longest x36 42.6 us: xor_send(): lax.ppermute(value, 'blk', [(i, i ^ 2 * k) for i in range(block_count)])]
    reshape x0 -> x49, local copies, waits for them, and re-layouts: none -> 38.1 us  [the longest x6 7.86 us: one_walker(): mm('acb,bx->acx', chosen, keys).astype(BF).reshape(2, slots * rows, width)]
    mul x0 -> x48, local copies, waits for them, and re-layouts: none -> 30.4 us  [the longest x24 20.2 us: attend(): qm = (q[None] * masks).reshape(heads * rows, -1)]
    dot_general x315 -> x234, matrix products: 184 us -> 206 us  [mm(): return jnp.einsum(spec, *args, preferred_element_type=F32)]
    while x252 -> x48, local copies, waits for them, and re-layouts: 0.65 us -> 19.1 us
  transfers between devices with their start and end apart: 19 -> 45, of which waited for: 19 -> 10; matrix products, arithmetic and copies ran while one was open for 5% -> 29% of each run, Pallas kernels for 0% -> 0%
where the time goes in v1:
time: 507 us; the launch traced here: 497 us
  matrix products  206 us (41%)
  local copies, waits for them, and re-layouts  148 us (29%)
  starting transfers between devices  58.9 us (12%)
  other arithmetic  48.3 us (10%)
  waiting for transfers between devices  22.3 us (4%)
  blocking collectives  8.88 us (2%)
    dot_general x234, matrix products, mm(): return jnp.einsum(spec, *args, preferred_element_type=F32)  206 us
    ppermute x36, starting transfers between devices, xor_send(): lax.ppermute(value, 'blk', [(i, i ^ 2 * k) for i in range(block_count)])  42.6 us
    mul x24, local copies, waits for them, and re-layouts, attend(): qm = (q[None] * masks).reshape(heads * rows, -1)  20.2 us
    while x48, local copies, waits for them, and re-layouts  19.1 us
    broadcast_in_dim x25, local copies, waits for them, and re-layouts, one_walker(): jnp.repeat(arg, parts, axis=0)  19.1 us
    convert_element_type x24, other arithmetic, attend(): wide = masks.astype(F32)  16.3 us
    dynamic_update_slice x24, local copies, waits for them, and re-layouts, one_walker(): lax.map(one, tuple(args))  16 us
    ppermute x5, starting transfers between devices, per_device(): lax.ppermute(input_grad, 'segment', [(i, (i - 1) % segments) for i in ran...  12 us
  transfers between devices with their start and end apart: 45, of which 10 were waited for; matrix products, arithmetic and copies ran while one was open for 29% of the time, Pallas kernels for 0%

profile of v1, /device:TPU:0, one launch (start us, length us, event | category | flops | bytes accessed | tf_op | source)
XLA Modules:
  0.0 497.3 jit_solution(876377122835839486)
XLA Ops:
  7.3 2.9 collective-permute-start.2
  28.5 39.6 %while.96 = (s32[]{:T(128)}, bf16[4,128,256]{2,1,0:T(8,128)(2,1)}, bf16[4,128,256]{2,1,0:T(8,128)(2,1)}, bf16[4,512,256]{2,1,0:T(8,128)(2,1)S(1)}, bf16[4,512,25...) while((s32[]{:T(128)}, bf16[4,128,256]{2,1,0:T(8,128)(2,1)}, ...), condition=%wide.region_6.7_spmd, body=%wide.region_1.6_spmd.sunk | while | flops 1620803584 | bytes 22741168 | solution.py:104
  82.8 1.8 fusion.192
  89.0 1.8 collective-permute-start.11
  93.2 2.9 collective-permute-done.17
  101.5 3.6 collective-permute-start.8
  107.4 2.0 convolution_convert_fusion.33
  114.5 1.6 collective-permute-start.31
  122.2 39.3 %while.97 = (s32[]{:T(128)}, bf16[4,128,256]{2,1,0:T(8,128)(2,1)}, bf16[4,128,256]{2,1,0:T(8,128)(2,1)}, bf16[4,512,256]{2,1,0:T(8,128)(2,1)S(1)}, bf16[4,512,25...) while((s32[]{:T(128)}, bf16[4,128,256]{2,1,0:T(8,128)(2,1)}, ...), condition=%wide.region_17.18_spmd, body=%wide.region_12.17_spmd.sunk | while | flops 1620803584 | bytes 22741168 | solution.py:104
  124.7 1.6 fusion.707
  144.3 1.6 fusion.707
  175.1 1.6 collective-permute-start.38
  176.8 2.2 convolution_convert_fusion.28
  181.5 2.2 convolution_convert_fusion.29
  190.0 1.6 collective-permute-start.13
  201.4 2.3 convolution_convert_fusion.24
  206.1 2.1 convolution_bitcast_fusion.21
  210.4 1.9 fusion.202
  217.0 2.3 reshape.1226
  219.2 2.2 reshape.1247
  222.7 2.2 reshape.1262
  224.9 2.2 reshape.1265
  233.2 39.1 %while.98 = (s32[]{:T(128)}, bf16[4,128,256]{2,1,0:T(8,128)(2,1)}, bf16[4,128,256]{2,1,0:T(8,128)(2,1)}, bf16[4,512,256]{2,1,0:T(8,128)(2,1)S(1)}, bf16[4,512,25...) while((s32[]{:T(128)}, bf16[4,128,256]{2,1,0:T(8,128)(2,1)}, ...), condition=%wide.region_28.29_spmd, body=%wide.region_23.28_spmd.sunk | while | flops 1620803584 | bytes 22741168 | solution.py:104
  282.1 1.7 collective-permute-start.20
  293.0 2.9 collective-permute-done.22
  301.3 35.8 %while.99 = (s32[]{:T(128)}, bf16[4,128,256]{2,1,0:T(8,128)(2,1)}, bf16[4,128,256]{2,1,0:T(8,128)(2,1)}, bf16[4,512,256]{2,1,0:T(8,128)(2,1)S(1)}, bf16[4,512,25...) while((s32[]{:T(128)}, bf16[4,128,256]{2,1,0:T(8,128)(2,1)}, ...), condition=%wide.region_39.40_spmd, body=%wide.region_34.39_spmd.sunk | while | flops 1620803584 | bytes 22741168 | solution.py:104
  302.9 1.6 fusion.743
  311.8 1.6 fusion.743
  329.7 1.6 fusion.743
  342.6 1.9 collective-permute-start.28
  344.5 2.2 convolution_bitcast_fusion.17
  346.7 2.2 convolution_bitcast_fusion.16
  350.6 2.5 collective-permute-start.29
  361.2 35.8 %while.100 = (s32[]{:T(128)}, bf16[4,128,256]{2,1,0:T(8,128)(2,1)}, bf16[4,128,256]{2,1,0:T(8,128)(2,1)}, bf16[4,512,256]{2,1,0:T(8,128)(2,1)S(1)}, bf16[4,512,2...) while((s32[]{:T(128)}, bf16[4,128,256]{2,1,0:T(8,128)(2,1)}, ...), condition=%wide.region_50.51_spmd, body=%wide.region_45.50_spmd.sunk | while | flops 1620803584 | bytes 22741168 | solution.py:104
  371.7 1.6 fusion.761
  389.6 1.6 fusion.761
  402.5 1.9 collective-permute-start.35
  404.4 2.2 convolution_bitcast_fusion.15
  406.6 2.2 convolution_bitcast_fusion.14
  411.0 4.3 collective-permute-start.36
  423.3 35.8 %while.101 = (s32[]{:T(128)}, bf16[4,128,256]{2,1,0:T(8,128)(2,1)}, bf16[4,128,256]{2,1,0:T(8,128)(2,1)}, bf16[4,512,256]{2,1,0:T(8,128)(2,1)S(1)}, bf16[4,512,2...) while((s32[]{:T(128)}, bf16[4,128,256]{2,1,0:T(8,128)(2,1)}, ...), condition=%wide.region_61.62_spmd, body=%wide.region_56.61_spmd.sunk | while | flops 1620803584 | bytes 22741168 | solution.py:104
  424.9 1.6 fusion.779
  433.8 1.6 fusion.779
  451.7 1.6 fusion.779
  465.0 1.9 collective-permute-start.42
  472.5 3.5 all-to-all-start
  477.0 9.5 %all-to-all-done = bf16[8,144,256]{2,1,0:T(8,128)(2,1)S(1)} async-done(((bf16[8,144,256]{2,1,0:T(8,128)(2,1)}), bf16[8,144,256]{2,1,0:T(8,128)(2,1)S(1)}, u32[]{:S(2)}, u32[]{:S(2)}) %all-to-all-start) | async-done | bytes 589856 | tf_op jit(solution)/shard_map/all_to_all | solution.py:166
  487.1 8.9 %all_gather.3 = bf16[1024,256]{1,0:T(8,128)(2,1)S(1)} all-gather(bf16[128,256]{1,0:T(8,128)(2,1)S(1)} %slice.415), channel_id=1, replica_groups=mesh['segment'=4,'blk'=8] {'blk'}, dimensions={0}, use_global_device_ids=true | all-gather | bytes 589824 | tf_op jit(solution)/shard_map/all_gather | solution.py:168
  (993 shorter events, 388.5 us)
Async XLA Ops:
  1.7 4.2 collective-permute-start.1
  3.1 13.4 %collective-permute-start = (bf16[3,128,256]{2,1,0:T(8,128)(2,1)S(1)}, bf16[3,128,256]{2,1,0:T(8,128)(2,1)S(1)}, u32[]{:S(2)}, u32[]{:S(2)}) collective-permute-start(bf16[3,128,256]{2,1,0:T(8,128)(2,1)S(1)} %dynamic-slice_bitcast_fusion.20), channel_id=1, source_target_pairs={{0,1},{1,0},{2,3},{3,2},{4,5},{5,4},{6,7},{7,6},{8,9},{9,8},{10,11... | collective-permute-start | bytes 589832 | tf_op jit(solution)/shard_map/ppermute | solution.py:71
  7.1 75.7 %copy-start.1 = (bf16[1,256,256]{2,1,0:T(8,128)(2,1)}, bf16[1,256,256]{2,1,0:T(8,128)(2,1)S(1)}, u32[]{:S(2)}) copy-start(bf16[1,256,256]{2,1,0:T(8,128)(2,1)S(1)} %get-tuple-element.636) | copy-start | bytes 393220
  7.1 75.7 %copy-start.3 = (bf16[1,256,256]{2,1,0:T(8,128)(2,1)}, bf16[1,256,256]{2,1,0:T(8,128)(2,1)S(1)}, u32[]{:S(2)}) copy-start(bf16[1,256,256]{2,1,0:T(8,128)(2,1)S(1)} %get-tuple-element.634) | copy-start | bytes 393220
  7.1 75.7 %copy-start.5 = (bf16[1,256,256]{2,1,0:T(8,128)(2,1)}, bf16[1,256,256]{2,1,0:T(8,128)(2,1)S(1)}, u32[]{:S(2)}) copy-start(bf16[1,256,256]{2,1,0:T(8,128)(2,1)S(1)} %get-tuple-element.544) | copy-start | bytes 393220
  7.3 9.6 %collective-permute-start.2 = (bf16[256,256]{1,0:T(8,128)(2,1)S(1)}, bf16[256,256]{1,0:T(8,128)(2,1)S(1)}, u32[]{:S(2)}, u32[]{:S(2)}) collective-permute-start(bf16[256,256]{1,0:T(8,128)(2,1)S(1)} %fusion.186), channel_id=1, source_target_pairs={{0,2},{1,3},{2,0},{3,1},{4,6},{5,7},{6,4},{7,5},{8,10},{9,11},{10,... | collective-permute-start | bytes 393224 | tf_op jit(solution)/shard_map/ppermute | solution.py:82
  10.2 8.0 %collective-permute-start.3 = (bf16[256,256]{1,0:T(8,128)(2,1)S(1)}, bf16[256,256]{1,0:T(8,128)(2,1)S(1)}, u32[]{:S(2)}, u32[]{:S(2)}) collective-permute-start(bf16[256,256]{1,0:T(8,128)(2,1)S(1)} %fusion.186), channel_id=1, source_target_pairs={{0,4},{1,5},{2,6},{3,7},{4,0},{5,1},{6,2},{7,3},{8,12},{9,13},{10,... | collective-permute-start | bytes 393224 | tf_op jit(solution)/shard_map/ppermute | solution.py:82
  11.8 6.5 %collective-permute-start.4 = (bf16[256,256]{1,0:T(8,128)(2,1)S(1)}, bf16[256,256]{1,0:T(8,128)(2,1)S(1)}, u32[]{:S(2)}, u32[]{:S(2)}) collective-permute-start(bf16[256,256]{1,0:T(8,128)(2,1)S(1)} %fusion.186), channel_id=1, source_target_pairs={{0,6},{1,7},{2,4},{3,5},{4,2},{5,3},{6,0},{7,1},{8,14},{9,15},{10,... | collective-permute-start | bytes 393224 | tf_op jit(solution)/shard_map/ppermute | solution.py:82
  74.2 7.7 %collective-permute-start.5 = (bf16[256,256]{1,0:T(8,128)(2,1)S(1)}, bf16[256,256]{1,0:T(8,128)(2,1)S(1)}, u32[]{:S(2)}, u32[]{:S(2)}) collective-permute-start(bf16[256,256]{1,0:T(8,128)(2,1)S(1)} %get-tuple-element.624), channel_id=1, source_target_pairs={{0,2},{1,3},{2,0},{3,1},{4,6},{5,7},{6,4},{7,5},{8,10},{9,11},{10,... | collective-permute-start | bytes 393224 | tf_op jit(solution)/shard_map/ppermute | solution.py:82
  74.9 7.1 %collective-permute-start.6 = (bf16[256,256]{1,0:T(8,128)(2,1)S(1)}, bf16[256,256]{1,0:T(8,128)(2,1)S(1)}, u32[]{:S(2)}, u32[]{:S(2)}) collective-permute-start(bf16[256,256]{1,0:T(8,128)(2,1)S(1)} %get-tuple-element.626), channel_id=1, source_target_pairs={{0,4},{1,5},{2,6},{3,7},{4,0},{5,1},{6,2},{7,3},{8,12},{9,13},{10,... | collective-permute-start | bytes 393224 | tf_op jit(solution)/shard_map/ppermute | solution.py:82
  76.4 6.4 %collective-permute-start.7 = (bf16[256,256]{1,0:T(8,128)(2,1)S(1)}, bf16[256,256]{1,0:T(8,128)(2,1)S(1)}, u32[]{:S(2)}, u32[]{:S(2)}) collective-permute-start(bf16[256,256]{1,0:T(8,128)(2,1)S(1)} %get-tuple-element.625), channel_id=1, source_target_pairs={{0,6},{1,7},{2,4},{3,5},{4,2},{5,3},{6,0},{7,1},{8,14},{9,15},{10,... | collective-permute-start | bytes 393224 | tf_op jit(solution)/shard_map/ppermute | solution.py:82
  84.7 7.7 %collective-permute-start.16 = (bf16[256,256]{1,0:T(8,128)(2,1)S(1)}, bf16[256,256]{1,0:T(8,128)(2,1)S(1)}, u32[]{:S(2)}, u32[]{:S(2)}) collective-permute-start(bf16[256,256]{1,0:T(8,128)(2,1)S(1)} %get-tuple-element.640), channel_id=1, source_target_pairs={{0,2},{1,3},{2,0},{3,1},{4,6},{5,7},{6,4},{7,5},{8,10},{9,11},{10,... | collective-permute-start | bytes 393224 | tf_op jit(solution)/shard_map/ppermute | solution.py:82
  85.9 10.2 %collective-permute-start.17 = (bf16[256,256]{1,0:T(8,128)(2,1)S(1)}, bf16[256,256]{1,0:T(8,128)(2,1)S(1)}, u32[]{:S(2)}, u32[]{:S(2)}) collective-permute-start(bf16[256,256]{1,0:T(8,128)(2,1)S(1)} %get-tuple-element.640), channel_id=1, source_target_pairs={{0,4},{1,5},{2,6},{3,7},{4,0},{5,1},{6,2},{7,3},{8,12},{9,13},{10,... | collective-permute-start | bytes 393224 | tf_op jit(solution)/shard_map/ppermute | solution.py:82
  86.8 10.0 %collective-permute-start.18 = (bf16[256,256]{1,0:T(8,128)(2,1)S(1)}, bf16[256,256]{1,0:T(8,128)(2,1)S(1)}, u32[]{:S(2)}, u32[]{:S(2)}) collective-permute-start(bf16[256,256]{1,0:T(8,128)(2,1)S(1)} %get-tuple-element.640), channel_id=1, source_target_pairs={{0,6},{1,7},{2,4},{3,5},{4,2},{5,3},{6,0},{7,1},{8,14},{9,15},{10,... | collective-permute-start | bytes 393224 | tf_op jit(solution)/shard_map/ppermute | solution.py:82
  88.1 12.2 %collective-permute-start.10 = (bf16[256,256]{1,0:T(8,128)(2,1)S(1)}, bf16[256,256]{1,0:T(8,128)(2,1)S(1)}, u32[]{:S(2)}, u32[]{:S(2)}) collective-permute-start(bf16[256,256]{1,0:T(8,128)(2,1)S(1)} %get-tuple-element.641), channel_id=1, source_target_pairs={{0,4},{1,5},{2,6},{3,7},{4,0},{5,1},{6,2},{7,3},{8,12},{9,13},{10,... | collective-permute-start | bytes 393224 | tf_op jit(solution)/shard_map/ppermute | solution.py:82
  89.0 12.5 %collective-permute-start.11 = (bf16[256,256]{1,0:T(8,128)(2,1)S(1)}, bf16[256,256]{1,0:T(8,128)(2,1)S(1)}, u32[]{:S(2)}, u32[]{:S(2)}) collective-permute-start(bf16[256,256]{1,0:T(8,128)(2,1)S(1)} %get-tuple-element.641), channel_id=1, source_target_pairs={{0,6},{1,7},{2,4},{3,5},{4,2},{5,3},{6,0},{7,1},{8,14},{9,15},{10,... | collective-permute-start | bytes 393224 | tf_op jit(solution)/shard_map/ppermute | solution.py:82
  92.4 12.8 %collective-permute-start.9 = (bf16[256,256]{1,0:T(8,128)(2,1)S(1)}, bf16[256,256]{1,0:T(8,128)(2,1)S(1)}, u32[]{:S(2)}, u32[]{:S(2)}) collective-permute-start(bf16[256,256]{1,0:T(8,128)(2,1)S(1)} %get-tuple-element.641), channel_id=1, source_target_pairs={{0,2},{1,3},{2,0},{3,1},{4,6},{5,7},{6,4},{7,5},{8,10},{9,11},{10,... | collective-permute-start | bytes 393224 | tf_op jit(solution)/shard_map/ppermute | solution.py:82
  96.1 77.2 %collective-permute-start.23 = (bf16[256,256]{1,0:T(8,128)(2,1)}, bf16[256,256]{1,0:T(8,128)(2,1)}, u32[]{:S(2)}, u32[]{:S(2)}) collective-permute-start(bf16[256,256]{1,0:T(8,128)(2,1)} %get-tuple-element.639), channel_id=1, source_target_pairs={{0,2},{1,3},{2,0},{3,1},{4,6},{5,7},{6,4},{7,5},{8,10},{9,11},{10,... | collective-permute-start | bytes 393224 | tf_op jit(solution)/shard_map/ppermute | solution.py:82
  96.7 77.6 %collective-permute-start.24 = (bf16[256,256]{1,0:T(8,128)(2,1)}, bf16[256,256]{1,0:T(8,128)(2,1)}, u32[]{:S(2)}, u32[]{:S(2)}) collective-permute-start(bf16[256,256]{1,0:T(8,128)(2,1)} %get-tuple-element.639), channel_id=1, source_target_pairs={{0,4},{1,5},{2,6},{3,7},{4,0},{5,1},{6,2},{7,3},{8,12},{9,13},{10,... | collective-permute-start | bytes 393224 | tf_op jit(solution)/shard_map/ppermute | solution.py:82
  100.3 74.8 %collective-permute-start.25 = (bf16[256,256]{1,0:T(8,128)(2,1)}, bf16[256,256]{1,0:T(8,128)(2,1)}, u32[]{:S(2)}, u32[]{:S(2)}) collective-permute-start(bf16[256,256]{1,0:T(8,128)(2,1)} %get-tuple-element.639), channel_id=1, source_target_pairs={{0,6},{1,7},{2,4},{3,5},{4,2},{5,3},{6,0},{7,1},{8,14},{9,15},{10,... | collective-permute-start | bytes 393224 | tf_op jit(solution)/shard_map/ppermute | solution.py:82
  101.5 13.0 %collective-permute-start.8 = (bf16[256,256]{1,0:T(8,128)(2,1)}, bf16[256,256]{1,0:T(8,128)(2,1)S(1)}, u32[]{:S(2)}, u32[]{:S(2)}) collective-permute-start(bf16[256,256]{1,0:T(8,128)(2,1)} %get-tuple-element.564), channel_id=1, source_target_pairs={{0,24},{8,0},{16,8},{24,16},{1,25},{9,1},{17,9},{25,17},{2,26},{10... | collective-permute-start | bytes 393224 | tf_op jit(solution)/shard_map/ppermute | solution.py:151
  105.2 83.0 %collective-permute-start.30 = (bf16[256,256]{1,0:T(8,128)(2,1)}, bf16[256,256]{1,0:T(8,128)(2,1)}, u32[]{:S(2)}, u32[]{:S(2)}) collective-permute-start(bf16[256,256]{1,0:T(8,128)(2,1)} %get-tuple-element.638), channel_id=1, source_target_pairs={{0,2},{1,3},{2,0},{3,1},{4,6},{5,7},{6,4},{7,5},{8,10},{9,11},{10,... | collective-permute-start | bytes 393224 | tf_op jit(solution)/shard_map/ppermute | solution.py:82
  114.5 74.8 %collective-permute-start.31 = (bf16[256,256]{1,0:T(8,128)(2,1)}, bf16[256,256]{1,0:T(8,128)(2,1)}, u32[]{:S(2)}, u32[]{:S(2)}) collective-permute-start(bf16[256,256]{1,0:T(8,128)(2,1)} %get-tuple-element.638), channel_id=1, source_target_pairs={{0,4},{1,5},{2,6},{3,7},{4,0},{5,1},{6,2},{7,3},{8,12},{9,13},{10,... | collective-permute-start | bytes 393224 | tf_op jit(solution)/shard_map/ppermute | solution.py:82
  173.3 16.7 %collective-permute-start.32 = (bf16[256,256]{1,0:T(8,128)(2,1)}, bf16[256,256]{1,0:T(8,128)(2,1)}, u32[]{:S(2)}, u32[]{:S(2)}) collective-permute-start(bf16[256,256]{1,0:T(8,128)(2,1)} %get-tuple-element.638), channel_id=1, source_target_pairs={{0,6},{1,7},{2,4},{3,5},{4,2},{5,3},{6,0},{7,1},{8,14},{9,15},{10,... | collective-permute-start | bytes 393224 | tf_op jit(solution)/shard_map/ppermute | solution.py:82
  174.4 23.0 %collective-permute-start.37 = (bf16[256,256]{1,0:T(8,128)(2,1)}, bf16[256,256]{1,0:T(8,128)(2,1)}, u32[]{:S(2)}, u32[]{:S(2)}) collective-permute-start(bf16[256,256]{1,0:T(8,128)(2,1)} %get-tuple-element.637), channel_id=1, source_target_pairs={{0,2},{1,3},{2,0},{3,1},{4,6},{5,7},{6,4},{7,5},{8,10},{9,11},{10,... | collective-permute-start | bytes 393224 | tf_op jit(solution)/shard_map/ppermute | solution.py:82
  175.1 23.4 %collective-permute-start.38 = (bf16[256,256]{1,0:T(8,128)(2,1)}, bf16[256,256]{1,0:T(8,128)(2,1)}, u32[]{:S(2)}, u32[]{:S(2)}) collective-permute-start(bf16[256,256]{1,0:T(8,128)(2,1)} %get-tuple-element.637), channel_id=1, source_target_pairs={{0,4},{1,5},{2,6},{3,7},{4,0},{5,1},{6,2},{7,3},{8,12},{9,13},{10,... | collective-permute-start | bytes 393224 | tf_op jit(solution)/shard_map/ppermute | solution.py:82
  188.2 10.4 %collective-permute-start.39 = (bf16[256,256]{1,0:T(8,128)(2,1)}, bf16[256,256]{1,0:T(8,128)(2,1)}, u32[]{:S(2)}, u32[]{:S(2)}) collective-permute-start(bf16[256,256]{1,0:T(8,128)(2,1)} %get-tuple-element.637), channel_id=1, source_target_pairs={{0,6},{1,7},{2,4},{3,5},{4,2},{5,3},{6,0},{7,1},{8,14},{9,15},{10,... | collective-permute-start | bytes 393224 | tf_op jit(solution)/shard_map/ppermute | solution.py:82
  189.3 21.1 %collective-permute-start.12 = (bf16[256,256]{1,0:T(8,128)(2,1)}, bf16[256,256]{1,0:T(8,128)(2,1)S(1)}, u32[]{:S(2)}, u32[]{:S(2)}) collective-permute-start(bf16[256,256]{1,0:T(8,128)(2,1)} %get-tuple-element.621), channel_id=1, source_target_pairs={{0,2},{1,3},{2,0},{3,1},{4,6},{5,7},{6,4},{7,5},{8,10},{9,11},{10,... | collective-permute-start | bytes 393224 | tf_op jit(solution)/shard_map/ppermute | solution.py:82
  190.0 20.4 %collective-permute-start.13 = (bf16[256,256]{1,0:T(8,128)(2,1)}, bf16[256,256]{1,0:T(8,128)(2,1)}, u32[]{:S(2)}, u32[]{:S(2)}) collective-permute-start(bf16[256,256]{1,0:T(8,128)(2,1)} %get-tuple-element.623), channel_id=1, source_target_pairs={{0,4},{1,5},{2,6},{3,7},{4,0},{5,1},{6,2},{7,3},{8,12},{9,13},{10,... | collective-permute-start | bytes 393224 | tf_op jit(solution)/shard_map/ppermute | solution.py:82
  197.4 13.0 %collective-permute-start.14 = (bf16[256,256]{1,0:T(8,128)(2,1)}, bf16[256,256]{1,0:T(8,128)(2,1)S(1)}, u32[]{:S(2)}, u32[]{:S(2)}) collective-permute-start(bf16[256,256]{1,0:T(8,128)(2,1)} %get-tuple-element.622), channel_id=1, source_target_pairs={{0,6},{1,7},{2,4},{3,5},{4,2},{5,3},{6,0},{7,1},{8,14},{9,15},{10,... | collective-permute-start | bytes 393224 | tf_op jit(solution)/shard_map/ppermute | solution.py:82
  213.2 14.6 %collective-permute-start.15 = (bf16[256,256]{1,0:T(8,128)(2,1)}, bf16[256,256]{1,0:T(8,128)(2,1)S(1)}, u32[]{:S(2)}, u32[]{:S(2)}) collective-permute-start(bf16[256,256]{1,0:T(8,128)(2,1)} %get-tuple-element.560), channel_id=1, source_target_pairs={{0,24},{8,0},{16,8},{24,16},{1,25},{9,1},{17,9},{25,17},{2,26},{10... | collective-permute-start | bytes 393224 | tf_op jit(solution)/shard_map/ppermute | solution.py:151
  281.3 6.8 %collective-permute-start.19 = (bf16[256,256]{1,0:T(8,128)(2,1)S(1)}, bf16[256,256]{1,0:T(8,128)(2,1)S(1)}, u32[]{:S(2)}, u32[]{:S(2)}) collective-permute-start(bf16[256,256]{1,0:T(8,128)(2,1)S(1)} %get-tuple-element.618), channel_id=1, source_target_pairs={{0,2},{1,3},{2,0},{3,1},{4,6},{5,7},{6,4},{7,5},{8,10},{9,11},{10,... | collective-permute-start | bytes 393224 | tf_op jit(solution)/shard_map/ppermute | solution.py:82
  282.1 6.0 %collective-permute-start.20 = (bf16[256,256]{1,0:T(8,128)(2,1)S(1)}, bf16[256,256]{1,0:T(8,128)(2,1)S(1)}, u32[]{:S(2)}, u32[]{:S(2)}) collective-permute-start(bf16[256,256]{1,0:T(8,128)(2,1)S(1)} %get-tuple-element.620), channel_id=1, source_target_pairs={{0,4},{1,5},{2,6},{3,7},{4,0},{5,1},{6,2},{7,3},{8,12},{9,13},{10,... | collective-permute-start | bytes 393224 | tf_op jit(solution)/shard_map/ppermute | solution.py:82
  283.8 5.9 %collective-permute-start.21 = (bf16[256,256]{1,0:T(8,128)(2,1)S(1)}, bf16[256,256]{1,0:T(8,128)(2,1)S(1)}, u32[]{:S(2)}, u32[]{:S(2)}) collective-permute-start(bf16[256,256]{1,0:T(8,128)(2,1)S(1)} %get-tuple-element.619), channel_id=1, source_target_pairs={{0,6},{1,7},{2,4},{3,5},{4,2},{5,3},{6,0},{7,1},{8,14},{9,15},{10,... | collective-permute-start | bytes 393224 | tf_op jit(solution)/shard_map/ppermute | solution.py:82
  290.7 5.2 %collective-permute-start.22 = (bf16[256,256]{1,0:T(8,128)(2,1)S(1)}, bf16[256,256]{1,0:T(8,128)(2,1)S(1)}, u32[]{:S(2)}, u32[]{:S(2)}) collective-permute-start(bf16[256,256]{1,0:T(8,128)(2,1)S(1)} %get-tuple-element.554), channel_id=1, source_target_pairs={{0,24},{8,0},{16,8},{24,16},{1,25},{9,1},{17,9},{25,17},{2,26},{10... | collective-permute-start | bytes 393224 | tf_op jit(solution)/shard_map/ppermute | solution.py:151
  340.9 9.1 %collective-permute-start.26 = (bf16[256,256]{1,0:T(8,128)(2,1)S(1)}, bf16[256,256]{1,0:T(8,128)(2,1)S(1)}, u32[]{:S(2)}, u32[]{:S(2)}) collective-permute-start(bf16[256,256]{1,0:T(8,128)(2,1)S(1)} %get-tuple-element.615), channel_id=1, source_target_pairs={{0,2},{1,3},{2,0},{3,1},{4,6},{5,7},{6,4},{7,5},{8,10},{9,11},{10,... | collective-permute-start | bytes 393224 | tf_op jit(solution)/shard_map/ppermute | solution.py:82
  342.1 7.9 %collective-permute-start.27 = (bf16[256,256]{1,0:T(8,128)(2,1)S(1)}, bf16[256,256]{1,0:T(8,128)(2,1)S(1)}, u32[]{:S(2)}, u32[]{:S(2)}) collective-permute-start(bf16[256,256]{1,0:T(8,128)(2,1)S(1)} %get-tuple-element.617), channel_id=1, source_target_pairs={{0,4},{1,5},{2,6},{3,7},{4,0},{5,1},{6,2},{7,3},{8,12},{9,13},{10,... | collective-permute-start | bytes 393224 | tf_op jit(solution)/shard_map/ppermute | solution.py:82
  342.6 7.4 %collective-permute-start.28 = (bf16[256,256]{1,0:T(8,128)(2,1)S(1)}, bf16[256,256]{1,0:T(8,128)(2,1)S(1)}, u32[]{:S(2)}, u32[]{:S(2)}) collective-permute-start(bf16[256,256]{1,0:T(8,128)(2,1)S(1)} %get-tuple-element.616), channel_id=1, source_target_pairs={{0,6},{1,7},{2,4},{3,5},{4,2},{5,3},{6,0},{7,1},{8,14},{9,15},{10,... | collective-permute-start | bytes 393224 | tf_op jit(solution)/shard_map/ppermute | solution.py:82
  350.6 5.2 %collective-permute-start.29 = (bf16[256,256]{1,0:T(8,128)(2,1)S(1)}, bf16[256,256]{1,0:T(8,128)(2,1)S(1)}, u32[]{:S(2)}, u32[]{:S(2)}) collective-permute-start(bf16[256,256]{1,0:T(8,128)(2,1)S(1)} %get-tuple-element.550), channel_id=1, source_target_pairs={{0,24},{8,0},{16,8},{24,16},{1,25},{9,1},{17,9},{25,17},{2,26},{10... | collective-permute-start | bytes 393224 | tf_op jit(solution)/shard_map/ppermute | solution.py:151
  400.8 9.1 %collective-permute-start.33 = (bf16[256,256]{1,0:T(8,128)(2,1)S(1)}, bf16[256,256]{1,0:T(8,128)(2,1)S(1)}, u32[]{:S(2)}, u32[]{:S(2)}) collective-permute-start(bf16[256,256]{1,0:T(8,128)(2,1)S(1)} %get-tuple-element.612), channel_id=1, source_target_pairs={{0,2},{1,3},{2,0},{3,1},{4,6},{5,7},{6,4},{7,5},{8,10},{9,11},{10,... | collective-permute-start | bytes 393224 | tf_op jit(solution)/shard_map/ppermute | solution.py:82
  402.0 7.9 %collective-permute-start.34 = (bf16[256,256]{1,0:T(8,128)(2,1)S(1)}, bf16[256,256]{1,0:T(8,128)(2,1)S(1)}, u32[]{:S(2)}, u32[]{:S(2)}) collective-permute-start(bf16[256,256]{1,0:T(8,128)(2,1)S(1)} %get-tuple-element.614), channel_id=1, source_target_pairs={{0,4},{1,5},{2,6},{3,7},{4,0},{5,1},{6,2},{7,3},{8,12},{9,13},{10,... | collective-permute-start | bytes 393224 | tf_op jit(solution)/shard_map/ppermute | solution.py:82
  402.5 7.4 %collective-permute-start.35 = (bf16[256,256]{1,0:T(8,128)(2,1)S(1)}, bf16[256,256]{1,0:T(8,128)(2,1)S(1)}, u32[]{:S(2)}, u32[]{:S(2)}) collective-permute-start(bf16[256,256]{1,0:T(8,128)(2,1)S(1)} %get-tuple-element.613), channel_id=1, source_target_pairs={{0,6},{1,7},{2,4},{3,5},{4,2},{5,3},{6,0},{7,1},{8,14},{9,15},{10,... | collective-permute-start | bytes 393224 | tf_op jit(solution)/shard_map/ppermute | solution.py:82
  411.0 6.9 %collective-permute-start.36 = (bf16[256,256]{1,0:T(8,128)(2,1)S(1)}, bf16[256,256]{1,0:T(8,128)(2,1)S(1)}, u32[]{:S(2)}, u32[]{:S(2)}) collective-permute-start(bf16[256,256]{1,0:T(8,128)(2,1)S(1)} %get-tuple-element.546), channel_id=1, source_target_pairs={{0,24},{8,0},{16,8},{24,16},{1,25},{9,1},{17,9},{25,17},{2,26},{10... | collective-permute-start | bytes 393224 | tf_op jit(solution)/shard_map/ppermute | solution.py:151
  463.1 7.5 %collective-permute-start.40 = (bf16[256,256]{1,0:T(8,128)(2,1)S(1)}, bf16[256,256]{1,0:T(8,128)(2,1)S(1)}, u32[]{:S(2)}, u32[]{:S(2)}) collective-permute-start(bf16[256,256]{1,0:T(8,128)(2,1)S(1)} %get-tuple-element.609), channel_id=1, source_target_pairs={{0,2},{1,3},{2,0},{3,1},{4,6},{5,7},{6,4},{7,5},{8,10},{9,11},{10,... | collective-permute-start | bytes 393224 | tf_op jit(solution)/shard_map/ppermute | solution.py:82
  464.3 6.3 %collective-permute-start.41 = (bf16[256,256]{1,0:T(8,128)(2,1)S(1)}, bf16[256,256]{1,0:T(8,128)(2,1)S(1)}, u32[]{:S(2)}, u32[]{:S(2)}) collective-permute-start(bf16[256,256]{1,0:T(8,128)(2,1)S(1)} %get-tuple-element.611), channel_id=1, source_target_pairs={{0,4},{1,5},{2,6},{3,7},{4,0},{5,1},{6,2},{7,3},{8,12},{9,13},{10,... | collective-permute-start | bytes 393224 | tf_op jit(solution)/shard_map/ppermute | solution.py:82
  465.0 5.9 %collective-permute-start.42 = (bf16[256,256]{1,0:T(8,128)(2,1)S(1)}, bf16[256,256]{1,0:T(8,128)(2,1)S(1)}, u32[]{:S(2)}, u32[]{:S(2)}) collective-permute-start(bf16[256,256]{1,0:T(8,128)(2,1)S(1)} %get-tuple-element.610), channel_id=1, source_target_pairs={{0,6},{1,7},{2,4},{3,5},{4,2},{5,3},{6,0},{7,1},{8,14},{9,15},{10,... | collective-permute-start | bytes 393224 | tf_op jit(solution)/shard_map/ppermute | solution.py:82
  471.5 4.6 collective-permute-start.43
  472.5 13.9 %all-to-all-start = ((bf16[8,144,256]{2,1,0:T(8,128)(2,1)}), bf16[8,144,256]{2,1,0:T(8,128)(2,1)S(1)}, u32[]{:S(2)}, u32[]{:S(2)}) async-start(bf16[8,144,256]{2,1,0:T(8,128)(2,1)} %pad_maximum_fusion), calls=%async_computation | async-start | bytes 1179648 | tf_op jit(solution)/shard_map/all_to_all | solution.py:166
  (152 other events, 657.0 us)

commit v2 on v1

--- a/solution.py
+++ b/solution.py
@@ -95,7 +95,7 @@
         keys = mm("acb,bx->acx", chosen, keys).astype(BF).reshape(2, slots * rows, width)
         values = mm("acb,bx->acx", chosen, values).astype(BF).reshape(2, slots * rows, width)
         out_grad = mm("rd,ed->re", g, w[3]).astype(BF).reshape(2, rows, width)
-        parts = 4 if slots > 4 else 2
+        parts = 4 if slots > 4 else 1
         one = partial(attend, heads=HEADS // parts, scale=head_size ** (-0.5))
         args = [jnp.repeat(arg, parts, axis=0) for arg in (queries, keys, values, out_grad, ok)]
         args.append(jnp.concatenate([masks.reshape(parts, HEADS // parts, 1, width)] * 2))

time: 507 us -> 364 us (0.72)
  local copies, waits for them, and re-layouts: 148 us -> 58.5 us
  matrix products: 206 us -> 172 us
  other arithmetic: 48.3 us -> 25 us
  waiting for transfers between devices: 22.3 us -> 31 us
    dot_general x234 -> x162, matrix products: 206 us -> 172 us  [mm(): return jnp.einsum(spec, *args, preferred_element_type=F32)]
    reshape x25 -> x0, local copies, waits for them, and re-layouts: 24.6 us -> none  [the longest x6 7.86 us: one_walker(): mm('acb,bx->acx', chosen, keys).astype(BF).reshape(2, slots * rows, width)]
    broadcast_in_dim x25 -> x0, local copies, waits for them, and re-layouts: 19.1 us -> none  [one_walker(): jnp.repeat(arg, parts, axis=0)]
    convert_element_type x24 -> x12, other arithmetic: 16.3 us -> 0.08 us  [attend(): wide = masks.astype(F32)]
    while x48 -> x60, local copies, waits for them, and re-layouts: 19.1 us -> 3.18 us
    dynamic_update_slice x24 -> x12, local copies, waits for them, and re-layouts: 16 us -> 0.2 us  [one_walker(): lax.map(one, tuple(args))]
    mul x24 -> x12, local copies, waits for them, and re-layouts: 20.2 us -> 5.35 us  [attend(): qm = (q[None] * masks).reshape(heads * rows, -1)]
    mul x24 -> x12, local copies, waits for them, and re-layouts: 10.2 us -> 1.84 us  [attend(): om = (out_grad[None] * masks).reshape(heads * rows, -1)]
  transfers between devices with their start and end apart: 45 -> 45, of which waited for: 10 -> 12; matrix products, arithmetic and copies ran while one was open for 29% -> 36% of each run, Pallas kernels for 0% -> 0%
where the time goes in v2:
time: 364 us; the launch traced here: 358 us
  matrix products  172 us (47%)
  local copies, waits for them, and re-layouts  58.5 us (16%)
  starting transfers between devices  56.3 us (15%)
  waiting for transfers between devices  31 us (9%)
  other arithmetic  25 us (7%)
  blocking collectives  8.9 us (2%)
    dot_general x162, matrix products, mm(): return jnp.einsum(spec, *args, preferred_element_type=F32)  172 us
    ppermute x36, starting transfers between devices, xor_send(): lax.ppermute(value, 'blk', [(i, i ^ 2 * k) for i in range(block_count)])  41.9 us
    another operation x12, local copies, waits for them, and re-layouts, one_walker(): jnp.repeat(arg, parts, axis=0)  14.4 us
    ppermute x36, waiting for transfers between devices, xor_send(): lax.ppermute(value, 'blk', [(i, i ^ 2 * k) for i in range(block_count)])  13.7 us
    convert_element_type x12, other arithmetic, attend(): probs_b = probs.astype(BF)  10.6 us
    ppermute x5, starting transfers between devices, per_device(): lax.ppermute(input_grad, 'segment', [(i, (i - 1) % segments) for i in ran...  10.2 us
    all_to_all x1, waiting for transfers between devices, per_device(): got = lax.all_to_all(jnp.concatenate([flat, extra], axis=1), 'blk', 0, 0)  9.5 us
    all_gather x1, blocking collectives, per_device(): grads = lax.all_gather(total[:-16].astype(BF), 'blk', axis=0, tiled=True)  8.9 us
  transfers between devices with their start and end apart: 45, of which 12 were waited for; matrix products, arithmetic and copies ran while one was open for 36% of the time, Pallas kernels for 0%

profile of v2, /device:TPU:0, one launch (start us, length us, event | category | flops | bytes accessed | tf_op | source)
XLA Modules:
  0.0 358.0 jit_solution(4387942245383997576)
XLA Ops:
  7.3 3.9 %collective-permute-start.4 = (bf16[256,256]{1,0:T(8,128)(2,1)S(1)}, bf16[256,256]{1,0:T(8,128)(2,1)S(1)}, u32[]{:S(2)}, u32[]{:S(2)}) collective-permute-start(bf16[256,256]{1,0:T(8,128)(2,1)S(1)} %fusion.174), channel_id=1, source_target_pairs={{0,6},{1,7},{2,4},{3,5},{4,2},{5,3},{6,0},{7,1},{8,14},{9,15},{10,... | collective-permute-start | bytes 393224 | tf_op jit(solution)/shard_map/ppermute | solution.py:82
  25.3 20.2 %while.96 = (s32[]{:T(128)}, bf16[2,128,256]{2,1,0:T(8,128)(2,1)S(1)}, bf16[2,128,256]{2,1,0:T(8,128)(2,1)S(1)}, bf16[2,512,256]{2,1,0:T(8,128)(2,1)S(1)}, bf16[...) while((s32[]{:T(128)}, ...), condition=%wide.region_6.7_spmd, body=%wide.region_1.6_spmd.sunk | while | flops 3241377792 | bytes 38529760 | solution.py:104
  37.5 1.9 fusion.665
  49.9 2.0 collective-permute-start.5
  56.5 2.3 collective-permute-done.7
  62.3 3.8 %collective-permute-start.8 = (bf16[256,256]{1,0:T(8,128)(2,1)S(1)}, bf16[256,256]{1,0:T(8,128)(2,1)S(1)}, u32[]{:S(2)}, u32[]{:S(2)}) collective-permute-start(bf16[256,256]{1,0:T(8,128)(2,1)S(1)} %get-tuple-element.564), channel_id=1, source_target_pairs={{0,24},{8,0},{16,8},{24,16},{1,25},{9,1},{17,9},{25,17},{2,26},{10... | collective-permute-start | bytes 393224 | tf_op jit(solution)/shard_map/ppermute | solution.py:151
  75.1 2.3 collective-permute-done.11
  77.9 5.7 %collective-permute-done.10 = bf16[256,256]{1,0:T(8,128)(2,1)S(1)} collective-permute-done((bf16[256,256]{1,0:T(8,128)(2,1)S(1)}, bf16[256,256]{1,0:T(8,128)(2,1)S(1)}, u32[]{:S(2)}, u32[]{:S(2)}) %collective-permute-start.10) | collective-permute-done | bytes 131104 | tf_op jit(solution)/shard_map/ppermute | solution.py:82
  83.6 2.0 collective-permute-start.16
  89.8 19.7 %while.97 = (s32[]{:T(128)}, bf16[2,128,256]{2,1,0:T(8,128)(2,1)}, bf16[2,128,256]{2,1,0:T(8,128)(2,1)S(1)}, bf16[2,512,256]{2,1,0:T(8,128)(2,1)S(1)}, bf16[2,51...) while((s32[]{:T(128)}, bf16[2,128,256]{2,1,0:T(8,128)(2,1)}, ...), condition=%wide.region_14.15_spmd, body=%wide.region_9.14_spmd.sunk | while | flops 3241377792 | bytes 41675572 | solution.py:104
  112.0 2.0 fusion.123
  122.6 2.2 convolution_convert_fusion.31
  124.8 2.1 reshape.1118
  126.9 2.2 convolution_convert_fusion.19
  132.6 2.2 convolution_convert_fusion.28
  134.8 2.1 reshape.1123
  136.9 2.2 convolution_convert_fusion.16
  139.1 2.2 convolution_convert_fusion.29
  141.3 2.1 reshape.1122
  143.4 2.3 convolution_convert_fusion.17
  147.8 1.9 collective-permute-start.12
  151.3 2.1 convolution_convert_fusion.26
  155.9 2.2 convolution_convert_fusion.27
  160.6 2.2 convolution_convert_fusion.24
  165.3 2.1 convolution_convert_fusion.25
  169.9 2.0 convolution_bitcast_fusion.20
  172.0 2.5 convolution_bitcast_fusion.21
  175.5 2.1 fusion.190
  184.9 2.2 reshape_broadcast_in_dim_reshape.99
  192.0 18.0 %while.98 = (s32[]{:T(128)}, bf16[2,128,256]{2,1,0:T(8,128)(2,1)S(1)}, bf16[2,128,256]{2,1,0:T(8,128)(2,1)S(1)}, bf16[2,512,256]{2,1,0:T(8,128)(2,1)S(1)}, bf16[...) while((s32[]{:T(128)}, ...), condition=%wide.region_22.23_spmd, body=%wide.region_17.22_spmd.sunk | while | flops 3241377792 | bytes 38529760 | solution.py:104
  213.1 2.0 collective-permute-start.19
  216.7 2.1 convolution_bitcast_fusion.18
  218.8 2.2 convolution_bitcast_fusion.19
  224.5 4.0 %collective-permute-done.22 = bf16[256,256]{1,0:T(8,128)(2,1)S(1)} collective-permute-done((bf16[256,256]{1,0:T(8,128)(2,1)S(1)}, bf16[256,256]{1,0:T(8,128)(2,1)S(1)}, u32[]{:S(2)}, u32[]{:S(2)}) %collective-permute-start.22) | collective-permute-done | bytes 131104 | tf_op jit(solution)/shard_map/ppermute | solution.py:151
  228.9 16.5 %while.99 = (s32[]{:T(128)}, bf16[2,128,256]{2,1,0:T(8,128)(2,1)S(1)}, bf16[2,128,256]{2,1,0:T(8,128)(2,1)S(1)}, bf16[2,512,256]{2,1,0:T(8,128)(2,1)S(1)}, bf16[...) while((s32[]{:T(128)}, ...), condition=%wide.region_30.31_spmd, body=%wide.region_25.30_spmd.sunk | while | flops 3241377792 | bytes 38529760 | solution.py:104
  237.5 1.9 fusion.713
  252.0 2.1 convolution_bitcast_fusion.16
  254.1 2.1 convolution_bitcast_fusion.17
  261.3 2.2 collective-permute-done.29
  263.9 16.6 %while.100 = (s32[]{:T(128)}, bf16[2,128,256]{2,1,0:T(8,128)(2,1)S(1)}, bf16[2,128,256]{2,1,0:T(8,128)(2,1)S(1)}, bf16[2,512,256]{2,1,0:T(8,128)(2,1)S(1)}, bf16...) while((s32[]{:T(128)}, ...), condition=%wide.region_38.39_spmd, body=%wide.region_33.38_spmd.sunk | while | flops 3241377792 | bytes 38529760 | solution.py:104
  287.7 2.1 convolution_bitcast_fusion.14
  289.8 2.1 convolution_bitcast_fusion.15
  293.5 3.6 %collective-permute-start.36 = (bf16[256,256]{1,0:T(8,128)(2,1)S(1)}, bf16[256,256]{1,0:T(8,128)(2,1)S(1)}, u32[]{:S(2)}, u32[]{:S(2)}) collective-permute-start(bf16[256,256]{1,0:T(8,128)(2,1)S(1)} %get-tuple-element.546), channel_id=1, source_target_pairs={{0,24},{8,0},{16,8},{24,16},{1,25},{9,1},{17,9},{25,17},{2,26},{10... | collective-permute-start | bytes 393224 | tf_op jit(solution)/shard_map/ppermute | solution.py:151
  300.1 16.6 %while.101 = (s32[]{:T(128)}, bf16[2,128,256]{2,1,0:T(8,128)(2,1)S(1)}, bf16[2,128,256]{2,1,0:T(8,128)(2,1)S(1)}, bf16[2,512,256]{2,1,0:T(8,128)(2,1)S(1)}, bf16...) while((s32[]{:T(128)}, ...), condition=%wide.region_46.47_spmd, body=%wide.region_41.46_spmd.sunk | while | flops 3241377792 | bytes 38529760 | solution.py:104
  308.8 1.9 fusion.745
  333.2 3.5 all-to-all-start
  337.6 9.5 %all-to-all-done = bf16[8,144,256]{2,1,0:T(8,128)(2,1)S(1)} async-done(((bf16[8,144,256]{2,1,0:T(8,128)(2,1)}), bf16[8,144,256]{2,1,0:T(8,128)(2,1)S(1)}, u32[]{:S(2)}, u32[]{:S(2)}) %all-to-all-start) | async-done | bytes 589856 | tf_op jit(solution)/shard_map/all_to_all | solution.py:166
  347.8 8.9 %all_gather.3 = bf16[1024,256]{1,0:T(8,128)(2,1)S(1)} all-gather(bf16[128,256]{1,0:T(8,128)(2,1)S(1)} %slice.415), channel_id=1, replica_groups=mesh['segment'=4,'blk'=8] {'blk'}, dimensions={0}, use_global_device_ids=true | all-gather | bytes 589824 | tf_op jit(solution)/shard_map/all_gather | solution.py:168
  (707 shorter events, 237.0 us)
Async XLA Ops:
  1.7 18.3 %collective-permute-start = (bf16[3,128,256]{2,1,0:T(8,128)(2,1)S(1)}, bf16[3,128,256]{2,1,0:T(8,128)(2,1)S(1)}, u32[]{:S(2)}, u32[]{:S(2)}) collective-permute-start(bf16[3,128,256]{2,1,0:T(8,128)(2,1)S(1)} %dynamic-slice_bitcast_fusion.20), channel_id=1, source_target_pairs={{0,1},{1,0},{2,3},{3,2},{4,5},{5,4},{6,7},{7,6},{8,9},{9,8},{10,11... | collective-permute-start | bytes 589832 | tf_op jit(solution)/shard_map/ppermute | solution.py:71
  3.2 2.0 collective-permute-start.1
  5.1 105.2 %copy-start.39 = (s32[2,4]{1,0:T(2,128)}, s32[2,4]{1,0:T(2,128)S(1)}, u32[]{:S(2)}) copy-start(s32[2,4]{1,0:T(2,128)S(1)} %copy.24) | copy-start | bytes 100
  6.4 53.8 %copy-start.1 = (bf16[1,256,256]{2,1,0:T(8,128)(2,1)}, bf16[1,256,256]{2,1,0:T(8,128)(2,1)S(1)}, u32[]{:S(2)}) copy-start(bf16[1,256,256]{2,1,0:T(8,128)(2,1)S(1)} %get-tuple-element.636) | copy-start | bytes 393220
  6.4 53.7 %copy-start.3 = (bf16[1,256,256]{2,1,0:T(8,128)(2,1)}, bf16[1,256,256]{2,1,0:T(8,128)(2,1)S(1)}, u32[]{:S(2)}) copy-start(bf16[1,256,256]{2,1,0:T(8,128)(2,1)S(1)} %get-tuple-element.634) | copy-start | bytes 393220
  7.3 13.6 %collective-permute-start.4 = (bf16[256,256]{1,0:T(8,128)(2,1)S(1)}, bf16[256,256]{1,0:T(8,128)(2,1)S(1)}, u32[]{:S(2)}, u32[]{:S(2)}) collective-permute-start(bf16[256,256]{1,0:T(8,128)(2,1)S(1)} %fusion.174), channel_id=1, source_target_pairs={{0,6},{1,7},{2,4},{3,5},{4,2},{5,3},{6,0},{7,1},{8,14},{9,15},{10,... | collective-permute-start | bytes 393224 | tf_op jit(solution)/shard_map/ppermute | solution.py:82
  11.2 9.7 %collective-permute-start.3 = (bf16[256,256]{1,0:T(8,128)(2,1)S(1)}, bf16[256,256]{1,0:T(8,128)(2,1)S(1)}, u32[]{:S(2)}, u32[]{:S(2)}) collective-permute-start(bf16[256,256]{1,0:T(8,128)(2,1)S(1)} %fusion.174), channel_id=1, source_target_pairs={{0,4},{1,5},{2,6},{3,7},{4,0},{5,1},{6,2},{7,3},{8,12},{9,13},{10,... | collective-permute-start | bytes 393224 | tf_op jit(solution)/shard_map/ppermute | solution.py:82
  11.7 9.2 %collective-permute-start.2 = (bf16[256,256]{1,0:T(8,128)(2,1)S(1)}, bf16[256,256]{1,0:T(8,128)(2,1)S(1)}, u32[]{:S(2)}, u32[]{:S(2)}) collective-permute-start(bf16[256,256]{1,0:T(8,128)(2,1)S(1)} %fusion.174), channel_id=1, source_target_pairs={{0,2},{1,3},{2,0},{3,1},{4,6},{5,7},{6,4},{7,5},{8,10},{9,11},{10,... | collective-permute-start | bytes 393224 | tf_op jit(solution)/shard_map/ppermute | solution.py:82
  49.9 6.7 %collective-permute-start.5 = (bf16[256,256]{1,0:T(8,128)(2,1)S(1)}, bf16[256,256]{1,0:T(8,128)(2,1)S(1)}, u32[]{:S(2)}, u32[]{:S(2)}) collective-permute-start(bf16[256,256]{1,0:T(8,128)(2,1)S(1)} %get-tuple-element.624), channel_id=1, source_target_pairs={{0,2},{1,3},{2,0},{3,1},{4,6},{5,7},{6,4},{7,5},{8,10},{9,11},{10,... | collective-permute-start | bytes 393224 | tf_op jit(solution)/shard_map/ppermute | solution.py:82
  51.8 7.0 %collective-permute-start.7 = (bf16[256,256]{1,0:T(8,128)(2,1)S(1)}, bf16[256,256]{1,0:T(8,128)(2,1)S(1)}, u32[]{:S(2)}, u32[]{:S(2)}) collective-permute-start(bf16[256,256]{1,0:T(8,128)(2,1)S(1)} %get-tuple-element.625), channel_id=1, source_target_pairs={{0,6},{1,7},{2,4},{3,5},{4,2},{5,3},{6,0},{7,1},{8,14},{9,15},{10,... | collective-permute-start | bytes 393224 | tf_op jit(solution)/shard_map/ppermute | solution.py:82
  53.3 6.8 %collective-permute-start.6 = (bf16[256,256]{1,0:T(8,128)(2,1)S(1)}, bf16[256,256]{1,0:T(8,128)(2,1)S(1)}, u32[]{:S(2)}, u32[]{:S(2)}) collective-permute-start(bf16[256,256]{1,0:T(8,128)(2,1)S(1)} %get-tuple-element.626), channel_id=1, source_target_pairs={{0,4},{1,5},{2,6},{3,7},{4,0},{5,1},{6,2},{7,3},{8,12},{9,13},{10,... | collective-permute-start | bytes 393224 | tf_op jit(solution)/shard_map/ppermute | solution.py:82
  62.3 10.4 %collective-permute-start.8 = (bf16[256,256]{1,0:T(8,128)(2,1)S(1)}, bf16[256,256]{1,0:T(8,128)(2,1)S(1)}, u32[]{:S(2)}, u32[]{:S(2)}) collective-permute-start(bf16[256,256]{1,0:T(8,128)(2,1)S(1)} %get-tuple-element.564), channel_id=1, source_target_pairs={{0,24},{8,0},{16,8},{24,16},{1,25},{9,1},{17,9},{25,17},{2,26},{10... | collective-permute-start | bytes 393224 | tf_op jit(solution)/shard_map/ppermute | solution.py:151
  67.1 93.4 %collective-permute-start.39 = (bf16[256,256]{1,0:T(8,128)(2,1)}, bf16[256,256]{1,0:T(8,128)(2,1)}, u32[]{:S(2)}, u32[]{:S(2)}) collective-permute-start(bf16[256,256]{1,0:T(8,128)(2,1)} %get-tuple-element.637), channel_id=1, source_target_pairs={{0,6},{1,7},{2,4},{3,5},{4,2},{5,3},{6,0},{7,1},{8,14},{9,15},{10,... | collective-permute-start | bytes 393224 | tf_op jit(solution)/shard_map/ppermute | solution.py:82
  68.5 92.1 %collective-permute-start.38 = (bf16[256,256]{1,0:T(8,128)(2,1)}, bf16[256,256]{1,0:T(8,128)(2,1)}, u32[]{:S(2)}, u32[]{:S(2)}) collective-permute-start(bf16[256,256]{1,0:T(8,128)(2,1)} %get-tuple-element.637), channel_id=1, source_target_pairs={{0,4},{1,5},{2,6},{3,7},{4,0},{5,1},{6,2},{7,3},{8,12},{9,13},{10,... | collective-permute-start | bytes 393224 | tf_op jit(solution)/shard_map/ppermute | solution.py:82
  70.0 7.4 %collective-permute-start.11 = (bf16[256,256]{1,0:T(8,128)(2,1)S(1)}, bf16[256,256]{1,0:T(8,128)(2,1)S(1)}, u32[]{:S(2)}, u32[]{:S(2)}) collective-permute-start(bf16[256,256]{1,0:T(8,128)(2,1)S(1)} %get-tuple-element.641), channel_id=1, source_target_pairs={{0,6},{1,7},{2,4},{3,5},{4,2},{5,3},{6,0},{7,1},{8,14},{9,15},{10,... | collective-permute-start | bytes 393224 | tf_op jit(solution)/shard_map/ppermute | solution.py:82
  70.6 13.0 %collective-permute-start.10 = (bf16[256,256]{1,0:T(8,128)(2,1)S(1)}, bf16[256,256]{1,0:T(8,128)(2,1)S(1)}, u32[]{:S(2)}, u32[]{:S(2)}) collective-permute-start(bf16[256,256]{1,0:T(8,128)(2,1)S(1)} %get-tuple-element.641), channel_id=1, source_target_pairs={{0,4},{1,5},{2,6},{3,7},{4,0},{5,1},{6,2},{7,3},{8,12},{9,13},{10,... | collective-permute-start | bytes 393224 | tf_op jit(solution)/shard_map/ppermute | solution.py:82
  72.7 10.9 %collective-permute-start.9 = (bf16[256,256]{1,0:T(8,128)(2,1)S(1)}, bf16[256,256]{1,0:T(8,128)(2,1)S(1)}, u32[]{:S(2)}, u32[]{:S(2)}) collective-permute-start(bf16[256,256]{1,0:T(8,128)(2,1)S(1)} %get-tuple-element.641), channel_id=1, source_target_pairs={{0,2},{1,3},{2,0},{3,1},{4,6},{5,7},{6,4},{7,5},{8,10},{9,11},{10,... | collective-permute-start | bytes 393224 | tf_op jit(solution)/shard_map/ppermute | solution.py:82
  77.4 37.8 %collective-permute-start.18 = (bf16[256,256]{1,0:T(8,128)(2,1)}, bf16[256,256]{1,0:T(8,128)(2,1)}, u32[]{:S(2)}, u32[]{:S(2)}) collective-permute-start(bf16[256,256]{1,0:T(8,128)(2,1)} %get-tuple-element.640), channel_id=1, source_target_pairs={{0,6},{1,7},{2,4},{3,5},{4,2},{5,3},{6,0},{7,1},{8,14},{9,15},{10,... | collective-permute-start | bytes 393224 | tf_op jit(solution)/shard_map/ppermute | solution.py:82
  83.6 33.2 %collective-permute-start.17 = (bf16[256,256]{1,0:T(8,128)(2,1)}, bf16[256,256]{1,0:T(8,128)(2,1)}, u32[]{:S(2)}, u32[]{:S(2)}) collective-permute-start(bf16[256,256]{1,0:T(8,128)(2,1)} %get-tuple-element.640), channel_id=1, source_target_pairs={{0,4},{1,5},{2,6},{3,7},{4,0},{5,1},{6,2},{7,3},{8,12},{9,13},{10,... | collective-permute-start | bytes 393224 | tf_op jit(solution)/shard_map/ppermute | solution.py:82
  83.6 33.3 %collective-permute-start.16 = (bf16[256,256]{1,0:T(8,128)(2,1)}, bf16[256,256]{1,0:T(8,128)(2,1)}, u32[]{:S(2)}, u32[]{:S(2)}) collective-permute-start(bf16[256,256]{1,0:T(8,128)(2,1)} %get-tuple-element.640), channel_id=1, source_target_pairs={{0,2},{1,3},{2,0},{3,1},{4,6},{5,7},{6,4},{7,5},{8,10},{9,11},{10,... | collective-permute-start | bytes 393224 | tf_op jit(solution)/shard_map/ppermute | solution.py:82
  115.2 13.9 %collective-permute-start.25 = (bf16[256,256]{1,0:T(8,128)(2,1)}, bf16[256,256]{1,0:T(8,128)(2,1)}, u32[]{:S(2)}, u32[]{:S(2)}) collective-permute-start(bf16[256,256]{1,0:T(8,128)(2,1)} %get-tuple-element.639), channel_id=1, source_target_pairs={{0,6},{1,7},{2,4},{3,5},{4,2},{5,3},{6,0},{7,1},{8,14},{9,15},{10,... | collective-permute-start | bytes 393224 | tf_op jit(solution)/shard_map/ppermute | solution.py:82
  116.8 13.8 %collective-permute-start.24 = (bf16[256,256]{1,0:T(8,128)(2,1)}, bf16[256,256]{1,0:T(8,128)(2,1)}, u32[]{:S(2)}, u32[]{:S(2)}) collective-permute-start(bf16[256,256]{1,0:T(8,128)(2,1)} %get-tuple-element.639), channel_id=1, source_target_pairs={{0,4},{1,5},{2,6},{3,7},{4,0},{5,1},{6,2},{7,3},{8,12},{9,13},{10,... | collective-permute-start | bytes 393224 | tf_op jit(solution)/shard_map/ppermute | solution.py:82
  116.9 13.8 %collective-permute-start.23 = (bf16[256,256]{1,0:T(8,128)(2,1)}, bf16[256,256]{1,0:T(8,128)(2,1)}, u32[]{:S(2)}, u32[]{:S(2)}) collective-permute-start(bf16[256,256]{1,0:T(8,128)(2,1)} %get-tuple-element.639), channel_id=1, source_target_pairs={{0,2},{1,3},{2,0},{3,1},{4,6},{5,7},{6,4},{7,5},{8,10},{9,11},{10,... | collective-permute-start | bytes 393224 | tf_op jit(solution)/shard_map/ppermute | solution.py:82
  129.1 18.6 %collective-permute-start.32 = (bf16[256,256]{1,0:T(8,128)(2,1)}, bf16[256,256]{1,0:T(8,128)(2,1)}, u32[]{:S(2)}, u32[]{:S(2)}) collective-permute-start(bf16[256,256]{1,0:T(8,128)(2,1)} %get-tuple-element.638), channel_id=1, source_target_pairs={{0,6},{1,7},{2,4},{3,5},{4,2},{5,3},{6,0},{7,1},{8,14},{9,15},{10,... | collective-permute-start | bytes 393224 | tf_op jit(solution)/shard_map/ppermute | solution.py:82
  130.6 17.2 %collective-permute-start.31 = (bf16[256,256]{1,0:T(8,128)(2,1)}, bf16[256,256]{1,0:T(8,128)(2,1)}, u32[]{:S(2)}, u32[]{:S(2)}) collective-permute-start(bf16[256,256]{1,0:T(8,128)(2,1)} %get-tuple-element.638), channel_id=1, source_target_pairs={{0,4},{1,5},{2,6},{3,7},{4,0},{5,1},{6,2},{7,3},{8,12},{9,13},{10,... | collective-permute-start | bytes 393224 | tf_op jit(solution)/shard_map/ppermute | solution.py:82
  130.7 19.1 %collective-permute-start.30 = (bf16[256,256]{1,0:T(8,128)(2,1)}, bf16[256,256]{1,0:T(8,128)(2,1)}, u32[]{:S(2)}, u32[]{:S(2)}) collective-permute-start(bf16[256,256]{1,0:T(8,128)(2,1)} %get-tuple-element.638), channel_id=1, source_target_pairs={{0,2},{1,3},{2,0},{3,1},{4,6},{5,7},{6,4},{7,5},{8,10},{9,11},{10,... | collective-permute-start | bytes 393224 | tf_op jit(solution)/shard_map/ppermute | solution.py:82
  147.7 12.8 %collective-permute-start.37 = (bf16[256,256]{1,0:T(8,128)(2,1)}, bf16[256,256]{1,0:T(8,128)(2,1)S(1)}, u32[]{:S(2)}, u32[]{:S(2)}) collective-permute-start(bf16[256,256]{1,0:T(8,128)(2,1)} %get-tuple-element.637), channel_id=1, source_target_pairs={{0,2},{1,3},{2,0},{3,1},{4,6},{5,7},{6,4},{7,5},{8,10},{9,11},{10,... | collective-permute-start | bytes 393224 | tf_op jit(solution)/shard_map/ppermute | solution.py:82
  147.8 27.6 %collective-permute-start.12 = (bf16[256,256]{1,0:T(8,128)(2,1)}, bf16[256,256]{1,0:T(8,128)(2,1)}, u32[]{:S(2)}, u32[]{:S(2)}) collective-permute-start(bf16[256,256]{1,0:T(8,128)(2,1)} %get-tuple-element.621), channel_id=1, source_target_pairs={{0,2},{1,3},{2,0},{3,1},{4,6},{5,7},{6,4},{7,5},{8,10},{9,11},{10,... | collective-permute-start | bytes 393224 | tf_op jit(solution)/shard_map/ppermute | solution.py:82
  149.8 25.7 %collective-permute-start.14 = (bf16[256,256]{1,0:T(8,128)(2,1)}, bf16[256,256]{1,0:T(8,128)(2,1)}, u32[]{:S(2)}, u32[]{:S(2)}) collective-permute-start(bf16[256,256]{1,0:T(8,128)(2,1)} %get-tuple-element.622), channel_id=1, source_target_pairs={{0,6},{1,7},{2,4},{3,5},{4,2},{5,3},{6,0},{7,1},{8,14},{9,15},{10,... | collective-permute-start | bytes 393224 | tf_op jit(solution)/shard_map/ppermute | solution.py:82
  160.5 15.0 %collective-permute-start.13 = (bf16[256,256]{1,0:T(8,128)(2,1)}, bf16[256,256]{1,0:T(8,128)(2,1)}, u32[]{:S(2)}, u32[]{:S(2)}) collective-permute-start(bf16[256,256]{1,0:T(8,128)(2,1)} %get-tuple-element.623), channel_id=1, source_target_pairs={{0,4},{1,5},{2,6},{3,7},{4,0},{5,1},{6,2},{7,3},{8,12},{9,13},{10,... | collective-permute-start | bytes 393224 | tf_op jit(solution)/shard_map/ppermute | solution.py:82
  178.4 12.3 %collective-permute-start.15 = (bf16[256,256]{1,0:T(8,128)(2,1)}, bf16[256,256]{1,0:T(8,128)(2,1)}, u32[]{:S(2)}, u32[]{:S(2)}) collective-permute-start(bf16[256,256]{1,0:T(8,128)(2,1)} %get-tuple-element.560), channel_id=1, source_target_pairs={{0,24},{8,0},{16,8},{24,16},{1,25},{9,1},{17,9},{25,17},{2,26},{10... | collective-permute-start | bytes 393224 | tf_op jit(solution)/shard_map/ppermute | solution.py:151
  213.1 8.9 %collective-permute-start.19 = (bf16[256,256]{1,0:T(8,128)(2,1)S(1)}, bf16[256,256]{1,0:T(8,128)(2,1)S(1)}, u32[]{:S(2)}, u32[]{:S(2)}) collective-permute-start(bf16[256,256]{1,0:T(8,128)(2,1)S(1)} %get-tuple-element.618), channel_id=1, source_target_pairs={{0,2},{1,3},{2,0},{3,1},{4,6},{5,7},{6,4},{7,5},{8,10},{9,11},{10,... | collective-permute-start | bytes 393224 | tf_op jit(solution)/shard_map/ppermute | solution.py:82
  215.1 6.9 %collective-permute-start.21 = (bf16[256,256]{1,0:T(8,128)(2,1)S(1)}, bf16[256,256]{1,0:T(8,128)(2,1)S(1)}, u32[]{:S(2)}, u32[]{:S(2)}) collective-permute-start(bf16[256,256]{1,0:T(8,128)(2,1)S(1)} %get-tuple-element.619), channel_id=1, source_target_pairs={{0,6},{1,7},{2,4},{3,5},{4,2},{5,3},{6,0},{7,1},{8,14},{9,15},{10,... | collective-permute-start | bytes 393224 | tf_op jit(solution)/shard_map/ppermute | solution.py:82
  216.6 5.8 %collective-permute-start.20 = (bf16[256,256]{1,0:T(8,128)(2,1)S(1)}, bf16[256,256]{1,0:T(8,128)(2,1)S(1)}, u32[]{:S(2)}, u32[]{:S(2)}) collective-permute-start(bf16[256,256]{1,0:T(8,128)(2,1)S(1)} %get-tuple-element.620), channel_id=1, source_target_pairs={{0,4},{1,5},{2,6},{3,7},{4,0},{5,1},{6,2},{7,3},{8,12},{9,13},{10,... | collective-permute-start | bytes 393224 | tf_op jit(solution)/shard_map/ppermute | solution.py:82
  223.4 5.0 %collective-permute-start.22 = (bf16[256,256]{1,0:T(8,128)(2,1)S(1)}, bf16[256,256]{1,0:T(8,128)(2,1)S(1)}, u32[]{:S(2)}, u32[]{:S(2)}) collective-permute-start(bf16[256,256]{1,0:T(8,128)(2,1)S(1)} %get-tuple-element.554), channel_id=1, source_target_pairs={{0,24},{8,0},{16,8},{24,16},{1,25},{9,1},{17,9},{25,17},{2,26},{10... | collective-permute-start | bytes 393224 | tf_op jit(solution)/shard_map/ppermute | solution.py:151
  248.5 8.8 %collective-permute-start.26 = (bf16[256,256]{1,0:T(8,128)(2,1)S(1)}, bf16[256,256]{1,0:T(8,128)(2,1)S(1)}, u32[]{:S(2)}, u32[]{:S(2)}) collective-permute-start(bf16[256,256]{1,0:T(8,128)(2,1)S(1)} %get-tuple-element.615), channel_id=1, source_target_pairs={{0,2},{1,3},{2,0},{3,1},{4,6},{5,7},{6,4},{7,5},{8,10},{9,11},{10,... | collective-permute-start | bytes 393224 | tf_op jit(solution)/shard_map/ppermute | solution.py:82
  250.1 7.1 %collective-permute-start.28 = (bf16[256,256]{1,0:T(8,128)(2,1)S(1)}, bf16[256,256]{1,0:T(8,128)(2,1)S(1)}, u32[]{:S(2)}, u32[]{:S(2)}) collective-permute-start(bf16[256,256]{1,0:T(8,128)(2,1)S(1)} %get-tuple-element.616), channel_id=1, source_target_pairs={{0,6},{1,7},{2,4},{3,5},{4,2},{5,3},{6,0},{7,1},{8,14},{9,15},{10,... | collective-permute-start | bytes 393224 | tf_op jit(solution)/shard_map/ppermute | solution.py:82
  251.6 5.8 %collective-permute-start.27 = (bf16[256,256]{1,0:T(8,128)(2,1)S(1)}, bf16[256,256]{1,0:T(8,128)(2,1)S(1)}, u32[]{:S(2)}, u32[]{:S(2)}) collective-permute-start(bf16[256,256]{1,0:T(8,128)(2,1)S(1)} %get-tuple-element.617), channel_id=1, source_target_pairs={{0,4},{1,5},{2,6},{3,7},{4,0},{5,1},{6,2},{7,3},{8,12},{9,13},{10,... | collective-permute-start | bytes 393224 | tf_op jit(solution)/shard_map/ppermute | solution.py:82
  258.5 5.0 %collective-permute-start.29 = (bf16[256,256]{1,0:T(8,128)(2,1)S(1)}, bf16[256,256]{1,0:T(8,128)(2,1)S(1)}, u32[]{:S(2)}, u32[]{:S(2)}) collective-permute-start(bf16[256,256]{1,0:T(8,128)(2,1)S(1)} %get-tuple-element.550), channel_id=1, source_target_pairs={{0,24},{8,0},{16,8},{24,16},{1,25},{9,1},{17,9},{25,17},{2,26},{10... | collective-permute-start | bytes 393224 | tf_op jit(solution)/shard_map/ppermute | solution.py:151
  284.2 8.1 %collective-permute-start.33 = (bf16[256,256]{1,0:T(8,128)(2,1)S(1)}, bf16[256,256]{1,0:T(8,128)(2,1)S(1)}, u32[]{:S(2)}, u32[]{:S(2)}) collective-permute-start(bf16[256,256]{1,0:T(8,128)(2,1)S(1)} %get-tuple-element.612), channel_id=1, source_target_pairs={{0,2},{1,3},{2,0},{3,1},{4,6},{5,7},{6,4},{7,5},{8,10},{9,11},{10,... | collective-permute-start | bytes 393224 | tf_op jit(solution)/shard_map/ppermute | solution.py:82
  285.7 6.6 %collective-permute-start.35 = (bf16[256,256]{1,0:T(8,128)(2,1)S(1)}, bf16[256,256]{1,0:T(8,128)(2,1)S(1)}, u32[]{:S(2)}, u32[]{:S(2)}) collective-permute-start(bf16[256,256]{1,0:T(8,128)(2,1)S(1)} %get-tuple-element.613), channel_id=1, source_target_pairs={{0,6},{1,7},{2,4},{3,5},{4,2},{5,3},{6,0},{7,1},{8,14},{9,15},{10,... | collective-permute-start | bytes 393224 | tf_op jit(solution)/shard_map/ppermute | solution.py:82
  287.1 5.8 %collective-permute-start.34 = (bf16[256,256]{1,0:T(8,128)(2,1)S(1)}, bf16[256,256]{1,0:T(8,128)(2,1)S(1)}, u32[]{:S(2)}, u32[]{:S(2)}) collective-permute-start(bf16[256,256]{1,0:T(8,128)(2,1)S(1)} %get-tuple-element.614), channel_id=1, source_target_pairs={{0,4},{1,5},{2,6},{3,7},{4,0},{5,1},{6,2},{7,3},{8,12},{9,13},{10,... | collective-permute-start | bytes 393224 | tf_op jit(solution)/shard_map/ppermute | solution.py:82
  293.5 6.2 %collective-permute-start.36 = (bf16[256,256]{1,0:T(8,128)(2,1)S(1)}, bf16[256,256]{1,0:T(8,128)(2,1)S(1)}, u32[]{:S(2)}, u32[]{:S(2)}) collective-permute-start(bf16[256,256]{1,0:T(8,128)(2,1)S(1)} %get-tuple-element.546), channel_id=1, source_target_pairs={{0,24},{8,0},{16,8},{24,16},{1,25},{9,1},{17,9},{25,17},{2,26},{10... | collective-permute-start | bytes 393224 | tf_op jit(solution)/shard_map/ppermute | solution.py:151
  323.5 7.2 %collective-permute-start.40 = (bf16[256,256]{1,0:T(8,128)(2,1)S(1)}, bf16[256,256]{1,0:T(8,128)(2,1)S(1)}, u32[]{:S(2)}, u32[]{:S(2)}) collective-permute-start(bf16[256,256]{1,0:T(8,128)(2,1)S(1)} %get-tuple-element.609), channel_id=1, source_target_pairs={{0,2},{1,3},{2,0},{3,1},{4,6},{5,7},{6,4},{7,5},{8,10},{9,11},{10,... | collective-permute-start | bytes 393224 | tf_op jit(solution)/shard_map/ppermute | solution.py:82
  324.3 6.4 %collective-permute-start.42 = (bf16[256,256]{1,0:T(8,128)(2,1)S(1)}, bf16[256,256]{1,0:T(8,128)(2,1)S(1)}, u32[]{:S(2)}, u32[]{:S(2)}) collective-permute-start(bf16[256,256]{1,0:T(8,128)(2,1)S(1)} %get-tuple-element.610), channel_id=1, source_target_pairs={{0,6},{1,7},{2,4},{3,5},{4,2},{5,3},{6,0},{7,1},{8,14},{9,15},{10,... | collective-permute-start | bytes 393224 | tf_op jit(solution)/shard_map/ppermute | solution.py:82
  325.8 5.8 %collective-permute-start.41 = (bf16[256,256]{1,0:T(8,128)(2,1)S(1)}, bf16[256,256]{1,0:T(8,128)(2,1)S(1)}, u32[]{:S(2)}, u32[]{:S(2)}) collective-permute-start(bf16[256,256]{1,0:T(8,128)(2,1)S(1)} %get-tuple-element.611), channel_id=1, source_target_pairs={{0,4},{1,5},{2,6},{3,7},{4,0},{5,1},{6,2},{7,3},{8,12},{9,13},{10,... | collective-permute-start | bytes 393224 | tf_op jit(solution)/shard_map/ppermute | solution.py:82
  332.2 4.6 %collective-permute-start.43 = (bf16[3,128,256]{2,1,0:T(8,128)(2,1)S(1)}, bf16[3,128,256]{2,1,0:T(8,128)(2,1)S(1)}, u32[]{:S(2)}, u32[]{:S(2)}) collective-permute-start(bf16[3,128,256]{2,1,0:T(8,128)(2,1)S(1)} %dynamic-slice_bitcast_fusion.18), channel_id=1, source_target_pairs={{0,1},{1,0},{2,3},{3,2},{4,5},{5,4},{6,7},{7,6},{8,9},{9,8},{10,11... | collective-permute-start | bytes 589832 | tf_op jit(solution)/shard_map/ppermute | solution.py:157
  333.2 13.9 %all-to-all-start = ((bf16[8,144,256]{2,1,0:T(8,128)(2,1)}), bf16[8,144,256]{2,1,0:T(8,128)(2,1)S(1)}, u32[]{:S(2)}, u32[]{:S(2)}) async-start(bf16[8,144,256]{2,1,0:T(8,128)(2,1)} %pad_maximum_fusion), calls=%async_computation | async-start | bytes 1179648 | tf_op jit(solution)/shard_map/all_to_all | solution.py:166
  (124 other events, 1051.3 us)
